TPU v7x, 128 devices: a whole 4x4x4 slice. The times are simulated.
128 devices in a mesh: dp: 4 (over z), expert: 8 (over y, core), tensor: 4 (over x).
Axes of the slice: x: 4, y: 4, z: 4, core: 2. Of those that a mesh axis runs over, the one named last changes fastest.
Arguments:
- attn: bfloat16 [16384, 8192], P(('dp', 'expert'), 'tensor'), parts along dimension 0, may hold values from -6 to 6
- w_out: bfloat16 [8192, 5120], P('tensor', 'expert'), may hold values from -0.0625 to 0.0625
- resid: bfloat16 [16384, 5120], P(('dp', 'expert', 'tensor')), parts along dimension 0, may hold values from -40 to 40
- norm_gain: float32 [5120], replicated, may hold values from 0.1 to 1.9
- route_ids: int32 [16384, 1], P(('dp', 'expert', 'tensor')), parts along dimension 0, may hold values from 0 to 7, as said below
- gate_vals: float32 [16384, 1], P(('dp', 'expert', 'tensor')), parts along dimension 0, may hold values from 0.2 to 1
- w_gate: bfloat16 [8, 5120, 1536], P('expert', None, 'tensor'), may hold values from -0.078125 to 0.078125
- w_up: bfloat16 [8, 5120, 1536], P('expert', None, 'tensor'), may hold values from -0.078125 to 0.078125
- w_down: bfloat16 [8, 1536, 5120], P('expert', 'tensor'), may hold values from -0.15625 to 0.15625
Outputs:
- layer_out: bfloat16 [16384, 5120], P(('dp', 'expert', 'tensor')), parts along dimension 0
There are 4 independent parts, one for each index of `dp`. A program takes and returns all parts, laid end to end along the dimension named above; an argument that names none is the same for every part. Nothing has to cross between parts.
Inputs may be any that keep to these rules, and one draw needn't show every extreme that they name: `route_ids`: A row names 1 different experts. In each aligned block of 128 rows (the rows of one device) no expert is named by more than 24 rows, and one expert is named by exactly 24 rows in every block.
All inputs are finite; a program needn't handle non-finite values.
Results may differ from a plain program's by a relative error of at most 0.01.
Values may be sent and summed in bfloat16 or wider, within the bound.
A program may use at most 128 MiB of HBM per device.

v0:
```python
import jax
import jax.numpy as jnp
from jax import lax
from jax.sharding import PartitionSpec as P


def expert_rows(received, w_gate, w_up, w_down):
    layout = received.shape
    flat_rows = received.reshape(-1, layout[-1])
    gate_act = jnp.dot(flat_rows, w_gate[0], preferred_element_type=jnp.float32)
    up_act = jnp.dot(flat_rows, w_up[0], preferred_element_type=jnp.float32)
    activation = (jax.nn.silu(gate_act) * up_act).astype(jnp.bfloat16)
    down_part = jnp.dot(activation, w_down[0], preferred_element_type=jnp.float32).astype(
        jnp.bfloat16
    )
    return down_part.reshape(layout)


def shards(attn, w_out, resid, norm_gain, route_ids, gate_vals, w_gate, w_up, w_down):
    row_count = resid.shape[0]
    width_model = resid.shape[1]
    top_count = route_ids.shape[1]
    expert_count = lax.axis_size("expert")
    group_width = lax.axis_size("tensor")
    capacity = min(row_count, 3 * row_count * top_count // (2 * expert_count))
    projected = jnp.dot(
        attn,
        lax.all_gather(w_out, "expert", axis=1, tiled=True),
        preferred_element_type=jnp.float32,
    )
    summed = lax.psum_scatter(
        projected.astype(jnp.bfloat16), "tensor", scatter_dimension=0, tiled=True
    ).astype(jnp.float32)
    hidden = resid.astype(jnp.float32) + summed
    scale_inv = lax.rsqrt(jnp.mean(hidden * hidden, axis=1, keepdims=True) + 1e-06)
    normed = (hidden * scale_inv * norm_gain).astype(jnp.bfloat16)
    pair_ids = route_ids.reshape(-1)
    one_hot = (pair_ids[:, None] == jnp.arange(expert_count, dtype=jnp.int32)[None, :]).astype(
        jnp.int32
    )
    earlier = jnp.cumsum(one_hot, axis=0) - one_hot
    slot_index = jnp.sum(earlier * one_hot, axis=1)
    target = pair_ids * capacity + slot_index
    placed = (
        jnp.arange(expert_count * capacity, dtype=jnp.int32)[:, None] == target[None, :]
    ).astype(jnp.float32)
    placed_rows = placed.reshape(expert_count * capacity, row_count, top_count)
    dispatch = jnp.sum(placed_rows, axis=2)
    weights_comb = jnp.sum(placed_rows * gate_vals[None, :, :], axis=2)
    send_rows = jnp.dot(
        dispatch.astype(jnp.bfloat16), normed, preferred_element_type=jnp.float32
    ).astype(jnp.bfloat16)
    send_rows = send_rows.reshape(expert_count, capacity, width_model)
    copies = jnp.broadcast_to(
        send_rows[:, None], (expert_count, group_width, capacity, width_model)
    )
    copies = copies.reshape(expert_count * group_width, capacity, width_model)
    returned = lax.all_to_all(
        expert_rows(
            lax.all_to_all(copies, ("expert", "tensor"), split_axis=0, concat_axis=0, tiled=True),
            w_gate,
            w_up,
            w_down,
        ),
        ("expert", "tensor"),
        split_axis=0,
        concat_axis=0,
        tiled=True,
    )
    quarters = jnp.sum(
        returned.reshape(expert_count, group_width, capacity, width_model),
        axis=1,
        dtype=jnp.float32,
    )
    mixture = jnp.dot(
        weights_comb.T,
        quarters.reshape(expert_count * capacity, width_model),
        precision=lax.Precision.HIGHEST,
        preferred_element_type=jnp.float32,
    )
    return (hidden + mixture).astype(jnp.bfloat16)


def solution(mesh):
    placed = (
        P(("dp", "expert"), "tensor"),
        P("tensor", "expert"),
        P(("dp", "expert", "tensor"), None),
        P(),
        P(("dp", "expert", "tensor"), None),
        P(("dp", "expert", "tensor"), None),
        P("expert", None, "tensor"),
        P("expert", None, "tensor"),
        P("expert", "tensor", None),
    )
    return jax.shard_map(
        shards,
        mesh=mesh,
        in_specs=placed,
        out_specs=P(("dp", "expert", "tensor"), None),
        check_vma=False,
    )
```

profile of v0, /device:TPU:1, one launch (start us, length us, event | category | flops | bytes accessed | tf_op | source)
XLA Modules:
  0.0 417.1 jit_solution(12052089645430078061)
XLA Ops:
  6.5 0.0 copy-start
  6.5 0.7 all-gather.2.cloned.1.call-update
  7.3 0.0 reduce-scatter.2.cloned.1.call-start
  7.3 107.8 %all-gather.2.cloned.1.call-done = bf16[2048,5120]{1,0:T(8,128)(2,1)} async-done(((bf16[2048,640]{1,0:T(8,128)(2,1)}), bf16[2048,5120]{1,0:T(8,128)(2,1)}) %all-gather.2.cloned.1.call-update) | async-done | bytes 20971536 | tf_op jit(solution)/shard_map/all_gather | solution.py:28
  115.1 16.9 %convolution_convert_fusion.1 = bf16[512,5120]{1,0:T(8,128)(2,1)} fusion(bf16[512,2048]{1,0:T(8,128)(2,1)S(1)} %copy-done, bf16[2048,5120]{1,0:T(8,128)(2,1)} %all-gather.2.cloned.1.call-done), kind=kOutput, calls=%fused_computation.2 | convolution fusion | flops 10740039680 | bytes 28311552 | tf_op jit(solution)/shard_map/dot_general | solution.py:26
  132.0 0.0 reduce-scatter.2.cloned.1.call-update
  132.0 0.0 copy-start.6
  132.0 0.6 copy-done.7
  132.6 0.1 fusion.19
  132.7 0.2 reduce_window_sum.11
  132.9 0.2 select_reduce_fusion
  133.1 55.0 %reduce-scatter.2.cloned.1.call-done = bf16[128,5120]{1,0:T(8,128)(2,1)} async-done(((bf16[512,5120]{1,0:T(8,128)(2,1)}), bf16[128,5120]{1,0:T(8,128)(2,1)}) %reduce-scatter.2.cloned.1.call-update) | async-done | bytes 1310736 | tf_op jit(solution)/shard_map/reduce_scatter | solution.py:31
  188.0 1.9 multiply_reduce_fusion
  190.0 0.8 convolution_convert_fusion.2
  190.8 1.0 broadcast_in_dim.5
  191.8 0.0 copy-start.9
  191.8 96.1 %all_to_all.10 = bf16[32,24,5120]{2,1,0:T(8,128)(2,1)S(1)} all-to-all(bf16[32,24,5120]{2,1,0:T(8,128)(2,1)S(1)} %bitcast.34), channel_id=1, replica_groups=mesh['dp'=4,'expert'=8,'tensor'=4] {'expert','tensor'}, dimensions={0} | all-to-all | bytes 15728640 | tf_op jit(solution)/shard_map/all_to_all | solution.py:60
  287.9 3.1 copy-done.5
  291.0 4.2 %fusion.4 = f32[768,384]{1,0:T(8,128)S(1)} fusion(bf16[768,5120]{1,0:T(8,128)(2,1)S(1)} %bitcast.37, bf16[1,5120,384]{2,1,0:T(8,128)(2,1)S(1)} %copy-done.9), kind=kOutput, calls=%fused_computation.9 | convolution fusion | flops 3019898880 | bytes 12976128 | tf_op jit(solution)/shard_map/dot_general | solution.py:10
  295.2 15.0 %convolution_convert_fusion = bf16[768,5120]{1,0:T(8,128)(2,1)} fusion(bf16[1,384,5120]{2,1,0:T(8,128)(2,1)} %param.17, bf16[768,5120]{1,0:T(8,128)(2,1)} %bitcast.38, bf16[1,5120,384]{2,1,0:T(8,128)(2,1)} %param.16, f32[768,384]{1,0:T(8,128)S(1)} %fusion.4), kind=kOutput, calls=%fused_computation.1 | convolution fusion | flops 6045499392 | bytes 24772608 | tf_op jit(solution)/shard_map/dot_general | solution.py:13
  310.2 94.6 %all_to_all.11 = bf16[32,24,5120]{2,1,0:T(8,128)(2,1)S(1)} all-to-all(bf16[32,24,5120]{2,1,0:T(8,128)(2,1)} %bitcast.39), channel_id=1, replica_groups=mesh['dp'=4,'expert'=8,'tensor'=4] {'expert','tensor'}, dimensions={0} | all-to-all | bytes 15728640 | tf_op jit(solution)/shard_map/all_to_all | solution.py:58
  404.8 1.5 convert_reduce_fusion
  406.3 0.0 copy-start.1
  406.3 3.9 fusion
  (17 shorter events, 0.0 us)
Async XLA Ops:
  6.5 108.6 %copy-start = (bf16[512,2048]{1,0:T(8,128)(2,1)S(1)}, bf16[512,2048]{1,0:T(8,128)(2,1)}, u32[]{:S(2)}) copy-start(bf16[512,2048]{1,0:T(8,128)(2,1)} %param.9) | copy-start | bytes 6291460
  6.5 108.6 %all-gather.2.cloned.1.call-start = ((), (), s32[]{:S(2)}) async-start(), calls=%async_computation.3 | async-start | bytes 23592960 | tf_op jit(solution)/shard_map/all_gather | solution.py:28
  7.3 180.8 %reduce-scatter.2.cloned.1.call-start = ((), (), s32[]{:S(2)}) async-start(), calls=%async_computation.4 | async-start | bytes 6553600 | tf_op jit(solution)/shard_map/reduce_scatter | solution.py:31
  132.0 0.7 copy-start.7
  132.0 56.1 %copy-start.2 = (bf16[128,5120]{1,0:T(8,128)(2,1)S(1)}, bf16[128,5120]{1,0:T(8,128)(2,1)}, u32[]{:S(2)}) copy-start(bf16[128,5120]{1,0:T(8,128)(2,1)} %param.11) | copy-start | bytes 3932164
  132.0 58.0 %copy-start.6 = (f32[5120]{0:T(1024)S(1)}, f32[5120]{0:T(1024)}, u32[]{:S(2)}) copy-start(f32[5120]{0:T(1024)} %param.12) | copy-start | bytes 61444
  188.0 1.9 copy-start.3
  191.8 99.2 %copy-start.9 = (bf16[1,5120,384]{2,1,0:T(8,128)(2,1)S(1)}, bf16[1,5120,384]{2,1,0:T(8,128)(2,1)}, u32[]{:S(2)}) copy-start(bf16[1,5120,384]{2,1,0:T(8,128)(2,1)} %param.15) | copy-start | bytes 11796484
  287.9 3.1 copy-start.5
  404.8 1.5 copy-start.4
  404.8 1.5 copy-start.8
  406.3 3.9 copy-start.1
Sparse Core Ops, SparseCore 0:
  9.1 105.9 all-gather.1
  132.1 55.8 reduce-scatter.1
where the time goes:
time: 417 us
  blocking collectives  191 us (46%)
  waiting for transfers between devices  163 us (39%)
  matrix products  40.7 us (10%)
  between operations  13.5 us (3%)
  local copies, waits for them, and re-layouts  4.76 us (1%)
    all_gather x1, waiting for transfers between devices, shards(): lax.all_gather(w_out, 'expert', axis=1, tiled=True)  108 us
    all_to_all x1, blocking collectives, shards(): lax.all_to_all(copies, ('expert', 'tensor'), split_axis=0, concat_axis=0,...  96.1 us
    all_to_all x1, blocking collectives, shards(): lax.all_to_all(expert_rows(lax.all_to_all(copies, ('expert', 'tensor'), s...  94.6 us
    reduce_scatter x1, waiting for transfers between devices, shards(): lax.psum_scatter(projected.astype(jnp.bfloat16), 'tensor', scatter_dimens...  55 us
    dot_general x1, matrix products, shards(): jnp.dot(attn, lax.all_gather(w_out, 'expert', axis=1, tiled=True), prefer...  16.9 us
    dot_general x1, matrix products, expert_rows(): jnp.dot(activation, w_down[0], preferred_element_type=jnp.float32)  15 us
  transfers between devices with their start and end apart: 2, of which 2 were waited for; matrix products, arithmetic and copies ran while one was open for 0% of the time, Pallas kernels for 0%

commit v1 on v0

--- a/solution.py
+++ b/solution.py
@@ -1,18 +1,349 @@
+import functools
+
 import jax
 import jax.numpy as jnp
 from jax import lax
+from jax.experimental import pallas as pl
+from jax.experimental.pallas import tpu as pltpu
 from jax.sharding import PartitionSpec as P
+
+MESH = pl.DeviceIdType.MESH
+BF = jnp.bfloat16
+F32 = jnp.float32
+
+QN = 320
+DN = 2048 - 4 * QN
+WIDTHS = (256, 256, 128)
+OFFS = (0, 256, 512)
+STRIP = 640
+
+
+class Place:
+    def __init__(self):
+        self.z = lax.axis_index("dp")
+        self.e = lax.axis_index("expert")
+        self.x = lax.axis_index("tensor")
+        self.y = self.e // 2
+        self.c = self.e % 2
+
+    def at(self, dx=0, dy=0, dz=0, flip=False):
+        core = 1 - self.c if flip else self.c
+        return (
+            lax.rem(self.z + dz, 4),
+            lax.rem(self.y + dy, 4) * 2 + core,
+            lax.rem(self.x + dx, 4),
+        )
+
+
+class Links:
+    def __init__(self, send_sems, recv_sems):
+        self.send_sems, self.recv_sems, self.open = send_sems, recv_sems, []
+
+    def send(self, src, dst, device):
+        i = len(self.open)
+        copy = pltpu.make_async_remote_copy(
+            src_ref=src,
+            dst_ref=dst,
+            send_sem=self.send_sems.at[i],
+            recv_sem=self.recv_sems.at[i],
+            device_id=device,
+            device_id_type=MESH,
+        )
+        copy.start()
+        self.open.append(copy)
+        return copy
+
+    def drain(self):
+        for copy in self.open:
+            copy.wait_send()
+
+
+def greet(devices):
+    barrier = pltpu.get_barrier_semaphore()
+    for device in devices:
+        pl.semaphore_signal(barrier, inc=1, device_id=device, device_id_type=MESH)
+    pl.semaphore_wait(barrier, len(devices))
+
+
+A_SENDS = 96
+
+
+def project(
+    attn, w_out, resid, gain, hid_out,
+    a_buf, w_own, w0, w1, w2, res, hid,
+    p_own, p0, p1, p2, l_own, l0, l1, l2, f_own, f0, f1, f2,
+    ssq, ssq_sib, send_sems, recv_sems, local_sems,
+):
+    me = Place()
+    z, x, y, c = me.z, me.x, me.y, me.c
+    w = (w0, w1, w2)
+    parts = (p0, p1, p2)
+    relays = (l0, l1, l2)
+    finals = (f0, f1, f2)
+    sib = me.at(flip=True)
+    xp, xm, xo = me.at(dx=1), me.at(dx=3), me.at(dx=2)
+    yp, ym, zp, zm = me.at(dy=1), me.at(dy=3), me.at(dz=1), me.at(dz=3)
+    links = Links(send_sems, recv_sems)
+
+    load_w = pltpu.make_async_copy(w_out, w_own, local_sems.at[0])
+    load_w.start()
+    load_a = pltpu.make_async_copy(attn, a_buf.at[c], local_sems.at[1])
+    load_a.start()
+    load_r = []
+    for b in range(4):
+        col = pl.multiple_of((2 * b + c) * STRIP, 128)
+        load = pltpu.make_async_copy(
+            resid.at[:, pl.ds(col, STRIP)], res.at[c, :, pl.ds(b * STRIP, STRIP)], local_sems.at[2 + b]
+        )
+        load.start()
+        load_r.append(load)
+
+    greet([sib, yp, ym, zp, zm, xp, xm])
+
+    def rows_q(half=None):
+        start = z * QN
+        if half is None:
+            return pl.ds(pl.multiple_of(start, 16), QN)
+        return pl.ds(pl.multiple_of(start + half * (QN // 2), 16), QN // 2)
+
+    rows_d = pl.ds(4 * QN, DN)
+
+    def rows_dh(half):
+        return pl.ds(4 * QN + half * (DN // 2), DN // 2)
+
+    def own(j, rows):
+        return w_out.at[rows, pl.ds(OFFS[j], WIDTHS[j])]
+
+    def send_q(j):
+        return (
+            links.send(own(j, rows_q()), w[j].at[2, rows_q()], yp),
+            links.send(own(j, rows_q()), w[j].at[0, rows_q()], ym),
+        )
+
+    def send_d(j):
+        return (
+            links.send(own(j, rows_d), w[j].at[2, rows_d], yp),
+            links.send(own(j, rows_d), w[j].at[0, rows_d], ym),
+        )
+
+    n = len(WIDTHS)
+    q, d, rq, rd, zs, zo, zr = {}, {}, {}, {}, {}, {}, {}
+    q[0] = send_q(0)
+    sib_a = links.send(attn, a_buf.at[c], sib)
+    d[0] = send_d(0)
+    sib_r = []
+    for b in range(4):
+        col = pl.multiple_of((2 * b + 1 - c) * STRIP, 128)
+        sib_r.append(
+            links.send(resid.at[:, pl.ds(col, STRIP)], res.at[c, :, pl.ds(b * STRIP, STRIP)], sib)
+        )
+
+    def multiply(block, part, core, col, width):
+        def step(m, carry):
+            rows = pl.ds(pl.multiple_of(m * 256, 256), 256)
+            out = jnp.dot(a_buf[core, rows, :], block[...], preferred_element_type=F32).astype(BF)
+            part[2 * m, core, :, pl.ds(col, width)] = out[:128]
+            part[2 * m + 1, core, :, pl.ds(col, width)] = out[128:]
+            return carry
+
+        lax.fori_loop(0, 2, step, 0)
+
+    ahead, behind, over = lax.rem(x + 1, 4), lax.rem(x + 3, 4), lax.rem(x + 2, 4)
+
+    def reduce_first(part, relay, final):
+        return (
+            links.send(part.at[over, 0], relay.at[0], xp),
+            links.send(part.at[over, 1], relay.at[1], xm),
+            links.send(part.at[ahead, 1], final.at[0, 1], xp),
+            links.send(part.at[behind, 0], final.at[1, 0], xm),
+        )
+
+    def reduce_second(first, part, relay, final):
+        first[0].wait_recv()
+        part[ahead, 0] = (part[ahead, 0].astype(F32) + relay[0].astype(F32)).astype(BF)
+        one = links.send(part.at[ahead, 0], final.at[0, 0], xp)
+        first[1].wait_recv()
+        part[behind, 1] = (part[behind, 1].astype(F32) + relay[1].astype(F32)).astype(BF)
+        two = links.send(part.at[behind, 1], final.at[1, 1], xm)
+        return (first[2], first[3], one, two)
+
+    def on_q(j):
+        q[j][0].wait_recv()
+        one = links.send(w[j].at[2, rows_q(0)], w[j].at[1, rows_q(0)], yp)
+        z_a = (
+            links.send(w[j].at[2, rows_q()], w[j].at[2, rows_q()], zp),
+            links.send(w[j].at[2, rows_q()], w[j].at[2, rows_q()], zm),
+        )
+        q[j][1].wait_recv()
+        two = links.send(w[j].at[0, rows_q(1)], w[j].at[1, rows_q(1)], ym)
+        z_b = (
+            links.send(w[j].at[0, rows_q()], w[j].at[0, rows_q()], zp),
+            links.send(w[j].at[0, rows_q()], w[j].at[0, rows_q()], zm),
+        )
+        rq[j] = (one, two)
+        zs[j] = (z_a, z_b)
+        if j + 1 < n:
+            q[j + 1] = send_q(j + 1)
+
+    def on_rq(j):
+        rq[j][0].wait_recv()
+        rq[j][1].wait_recv()
+        zo[j] = (
+            links.send(w[j].at[1, rows_q()], w[j].at[1, rows_q()], zp),
+            links.send(w[j].at[1, rows_q()], w[j].at[1, rows_q()], zm),
+        )
+
+    def on_d(j):
+        d[j][0].wait_recv()
+        one = links.send(w[j].at[2, rows_dh(0)], w[j].at[1, rows_dh(0)], yp)
+        d[j][1].wait_recv()
+        two = links.send(w[j].at[0, rows_dh(1)], w[j].at[1, rows_dh(1)], ym)
+        rd[j] = (one, two)
+        if j + 1 < n:
+            d[j + 1] = send_d(j + 1)
+
+    def z_relay(j, pair, slot):
+        low = pl.ds(pl.multiple_of(lax.rem(z + 3, 4) * QN, 16), QN // 2)
+        high = pl.ds(pl.multiple_of(lax.rem(z + 1, 4) * QN + QN // 2, 16), QN // 2)
+        pair[0].wait_recv()
+        one = links.send(w[j].at[slot, low], w[j].at[slot, low], zp)
+        pair[1].wait_recv()
+        two = links.send(w[j].at[slot, high], w[j].at[slot, high], zm)
+        zr.setdefault(j, []).extend((one, two))
+
+    def on_z(j):
+        z_relay(j, zs[j][0], 2)
+        z_relay(j, zs[j][1], 0)
+
+    def on_zo(j):
+        z_relay(j, zo[j], 1)
+
+    def all_in(j):
+        for copy in rd[j]:
+            copy.wait_recv()
+        for copy in zr[j]:
+            copy.wait_recv()
+
+    def compute(j):
+        for slot in range(3):
+            for core in range(2):
+                multiply(w[j].at[slot], parts[j], core, slot * WIDTHS[j], WIDTHS[j])
+        return reduce_first(parts[j], relays[j], finals[j])
+
+    first, second = {}, {}
+    load_w.wait()
+    load_a.wait()
+    multiply(w_own, p_own, c, 0, STRIP)
+    sib_a.wait_recv()
+    multiply(w_own, p_own, 1 - c, 0, STRIP)
+    first["own"] = reduce_first(p_own, l_own, f_own)
+    on_q(0)
+    second["own"] = reduce_second(first["own"], p_own, l_own, f_own)
+
+    def finish(group, part, final, strips, width):
+        for copy in second[group]:
+            copy.wait_recv()
+        for k, (col, strip) in enumerate(strips):
+            cols = pl.ds(col, width)
+            for core in range(2):
+                at = pl.ds(k * width, width)
+                total = (
+                    res[core, :, cols].astype(F32)
+                    + part[x, core, :, at].astype(F32)
+                    + final[0, core, :, at].astype(F32)
+                    + final[1, core, :, at].astype(F32)
+                )
+                hid[core, :, cols] = total
+                add = jnp.sum(total * total, axis=1, keepdims=True)
+                ssq[core] = ssq[core] + jnp.broadcast_to(add, (128, 128))
+
+    ssq[...] = jnp.zeros_like(ssq)
+
+    def strips_of(j):
+        return [
+            (pl.multiple_of(lax.rem(y + 1 + slot, 4) * STRIP + OFFS[j], 128), slot)
+            for slot in range(3)
+        ]
+
+    on_rq(0)
+    for j in range(n):
+        on_d(j)
+        on_z(j)
+        on_zo(j)
+        if j + 1 < n:
+            on_q(j + 1)
+        if j == 0:
+            for load in load_r:
+                load.wait()
+            for copy in sib_r:
+                copy.wait_recv()
+            finish("own", p_own, f_own, [(pl.multiple_of(y * STRIP, 128), 0)], STRIP)
+        else:
+            second[j - 1] = reduce_second(first[j - 1], parts[j - 1], relays[j - 1], finals[j - 1])
+        all_in(j)
+        first[j] = compute(j)
+        if j + 1 < n:
+            on_rq(j + 1)
+        if j > 0:
+            finish(j - 1, parts[j - 1], finals[j - 1], strips_of(j - 1), WIDTHS[j - 1])
+    last = n - 1
+    second[last] = reduce_second(first[last], parts[last], relays[last], finals[last])
+    finish(last, parts[last], finals[last], strips_of(last), WIDTHS[last])
+
+    back = links.send(hid.at[1 - c], hid_out.at[c], sib)
+    keep = pltpu.make_async_copy(hid.at[c], hid_out.at[c], local_sems.at[6])
+    keep.start()
+    back.wait_recv()
+    keep.wait()
+    links.drain()
+
+
+def scratch_a():
+    def triple(shape):
+        return [pltpu.VMEM(shape(STRIP), BF)] + [pltpu.VMEM(shape(3 * v), BF) for v in WIDTHS]
+
+    return [
+        pltpu.VMEM((2, 512, 2048), BF),
+        pltpu.VMEM((2048, STRIP), BF),
+        *[pltpu.VMEM((3, 2048, v), BF) for v in WIDTHS],
+        pltpu.VMEM((2, 128, 4 * STRIP), BF),
+        pltpu.VMEM((2, 128, 4 * STRIP), F32),
+        *triple(lambda v: (4, 2, 128, v)),
+        *triple(lambda v: (2, 128, v)),
+        *triple(lambda v: (2, 2, 128, v)),
+        pltpu.VMEM((2, 128, 128), F32),
+        pltpu.VMEM((2, 128, 128), F32),
+        pltpu.SemaphoreType.DMA((A_SENDS,)),
+        pltpu.SemaphoreType.DMA((A_SENDS,)),
+        pltpu.SemaphoreType.DMA((8,)),
+    ]
+
+
+ANY = pl.BlockSpec(memory_space=pl.ANY)
+VM = pl.BlockSpec(memory_space=pltpu.VMEM)
+
+
+def call_a(attn, w_out, resid, gain):
+    return pl.pallas_call(
+        project,
+        out_shape=jax.ShapeDtypeStruct((2, 128, 4 * STRIP), F32),
+        in_specs=[ANY, ANY, ANY, VM],
+        out_specs=ANY,
+        scratch_shapes=scratch_a(),
+        compiler_params=pltpu.CompilerParams(
+            collective_id=0, has_side_effects=True, vmem_limit_bytes=56 * 2**20
+        ),
+        name="project",
+    )(attn, w_out, resid, gain)
 
 
 def expert_rows(received, w_gate, w_up, w_down):
     layout = received.shape
     flat_rows = received.reshape(-1, layout[-1])
-    gate_act = jnp.dot(flat_rows, w_gate[0], preferred_element_type=jnp.float32)
-    up_act = jnp.dot(flat_rows, w_up[0], preferred_element_type=jnp.float32)
-    activation = (jax.nn.silu(gate_act) * up_act).astype(jnp.bfloat16)
-    down_part = jnp.dot(activation, w_down[0], preferred_element_type=jnp.float32).astype(
-        jnp.bfloat16
-    )
+    gate_act = jnp.dot(flat_rows, w_gate[0], preferred_element_type=F32)
+    up_act = jnp.dot(flat_rows, w_up[0], preferred_element_type=F32)
+    activation = (jax.nn.silu(gate_act) * up_act).astype(BF)
+    down_part = jnp.dot(activation, w_down[0], preferred_element_type=F32).astype(BF)
     return down_part.reshape(layout)
 
 
@@ -23,15 +354,8 @@
     expert_count = lax.axis_size("expert")
     group_width = lax.axis_size("tensor")
     capacity = min(row_count, 3 * row_count * top_count // (2 * expert_count))
-    projected = jnp.dot(
-        attn,
-        lax.all_gather(w_out, "expert", axis=1, tiled=True),
-        preferred_element_type=jnp.float32,
-    )
-    summed = lax.psum_scatter(
-        projected.astype(jnp.bfloat16), "tensor", scatter_dimension=0, tiled=True
-    ).astype(jnp.float32)
-    hidden = resid.astype(jnp.float32) + summed
+    halves = call_a(attn, w_out, resid, norm_gain.reshape(1, -1))
+    hidden = halves.reshape(2, 128, 4, STRIP).transpose(1, 2, 0, 3).reshape(128, width_model)
     scale_inv = lax.rsqrt(jnp.mean(hidden * hidden, axis=1, keepdims=True) + 1e-06)
     normed = (hidden * scale_inv * norm_gain).astype(jnp.bfloat16)
     pair_ids = route_ids.reshape(-1)

time: 417 us -> 325 us (0.78)
  blocking collectives: 191 us -> 95.2 us
  Pallas kernels: 0 us -> 83.8 us
  waiting for transfers between devices: 163 us -> 90.4 us
  matrix products: 40.7 us -> 24.7 us
  between operations: 13.5 us -> 0.1 us
  local copies, waits for them, and re-layouts: 4.76 us -> 14.1 us
  other arithmetic: 3.82 us -> 9.33 us
  starting transfers between devices: 0.04 us -> 5.13 us
    all_gather x1 -> x0, waiting for transfers between devices: 108 us -> none  [shards(): lax.all_gather(w_out, 'expert', axis=1, tiled=True)]
    all_to_all x1 -> x0, blocking collectives: 94.6 us -> none  [shards(): lax.all_to_all(expert_rows(lax.all_to_all(copies, ('expert', 'tensor'), s...]
    all_to_all x0 -> x1, waiting for transfers between devices: none -> 90.4 us  [shards(): lax.all_to_all(expert_rows(lax.all_to_all(copies, ('expert', 'tensor'), s...]
    pallas_call x0 -> x1, Pallas kernels: none -> 83.8 us  [call_a(): pl.pallas_call(project, out_shape=jax.ShapeDtypeStruct((2, 128, 4 * STRIP...]
    reduce_scatter x1 -> x0, waiting for transfers between devices: 55 us -> none  [shards(): lax.psum_scatter(projected.astype(jnp.bfloat16), 'tensor', scatter_dimens...]
    dot_general x3 -> x2, matrix products: 36.1 us -> 20.4 us  [the longest x1 15.1 us: expert_rows(): jnp.dot(activation, w_down[0], preferred_element_type=F32).astype(BF)]
    reshape x0 -> x3, local copies, waits for them, and re-layouts: none -> 9.2 us  [shards(): halves.reshape(2, 128, 4, STRIP).transpose(1, 2, 0, 3)]
    all_to_all x0 -> x1, starting transfers between devices: none -> 5.13 us  [shards(): lax.all_to_all(expert_rows(lax.all_to_all(copies, ('expert', 'tensor'), s...]
  transfers between devices with their start and end apart: 2 -> 1, of which waited for: 2 -> 1; matrix products, arithmetic and copies ran while one was open for 0% -> 1% of each run, Pallas kernels for 0% -> 0%
where the time goes in v1:
time: 325 us; the launch traced here: 323 us
  blocking collectives  95.2 us (29%)
  waiting for transfers between devices  90.4 us (28%)
  Pallas kernels  83.8 us (26%)
  matrix products  24.7 us (8%)
  local copies, waits for them, and re-layouts  14.1 us (4%)
  other arithmetic  9.33 us (3%)
  starting transfers between devices  5.13 us (2%)
    all_to_all x1, blocking collectives, shards(): lax.all_to_all(copies, ('expert', 'tensor'), split_axis=0, concat_axis=0,...  95.2 us
    all_to_all x1, waiting for transfers between devices, shards(): lax.all_to_all(expert_rows(lax.all_to_all(copies, ('expert', 'tensor'), s...  90.4 us
    pallas_call x1, Pallas kernels, call_a(): pl.pallas_call(project, out_shape=jax.ShapeDtypeStruct((2, 128, 4 * STRIP...  83.8 us
    dot_general x1, matrix products, expert_rows(): jnp.dot(activation, w_down[0], preferred_element_type=F32).astype(BF)  15.1 us
    reshape x3, local copies, waits for them, and re-layouts, shards(): halves.reshape(2, 128, 4, STRIP).transpose(1, 2, 0, 3)  9.2 us
  transfers between devices with their start and end apart: 1, of which 1 were waited for; matrix products, arithmetic and copies ran while one was open for 1% of the time, Pallas kernels for 0%

profile of v1, /device:TPU:1, one launch (start us, length us, event | category | flops | bytes accessed | tf_op | source)
XLA Modules:
  0.0 322.8 jit_solution(752954383903242327)
XLA Ops:
  0.0 0.7 mul.67
  0.7 0.7 fusion.20
  1.5 0.2 reduce_window_sum.11
  1.7 0.8 select_reduce_fusion
  2.5 0.7 multiply_add_fusion
  3.2 83.8 %project.1 = f32[2,128,2560]{2,1,0:T(8,128)} custom-call(bf16[512,2048]{1,0:T(8,128)(2,1)} %attn.1, bf16[2048,640]{1,0:T(8,128)(2,1)} %w_out.1, bf16[128,5120]{1,0:T(8,128)(2,1)} %resid.1, f32[1,5120]{1,0:T(1,128)} %bitcast.54), custom_call_target="tpu_custom_call" | custom-call | tf_op jit(solution)/shard_map/project/pallas_call | solution.py:327
  87.0 4.0 %reshape.150 = f32[2,128,4,640]{3,2,1,0:T(4,128)} reshape(f32[2,128,2560]{2,1,0:T(8,128)} %project.1) | data formatting | bytes 5242880 | tf_op jit(solution)/shard_map/reshape | solution.py:358
  91.0 3.1 copy.11
  94.1 0.7 fusion.8
  94.8 1.0 fusion.7
  95.8 0.7 convolution_convert_fusion.1
  96.5 1.0 broadcast_in_dim.5
  97.5 0.0 copy-start.3
  97.5 95.2 %all_to_all.10 = bf16[32,24,5120]{2,1,0:T(8,128)(2,1)S(1)} all-to-all(bf16[32,24,5120]{2,1,0:T(8,128)(2,1)S(1)} %bitcast.47), channel_id=1, replica_groups=mesh['dp'=4,'expert'=8,'tensor'=4] {'expert','tensor'}, dimensions={0} | all-to-all | bytes 15728640 | tf_op jit(solution)/shard_map/all_to_all | solution.py:384
  192.7 3.2 copy-done.1
  195.9 0.0 copy-done.3
  195.9 5.3 %fusion.4 = f32[768,384]{1,0:T(8,128)} fusion(bf16[768,5120]{1,0:T(8,128)(2,1)S(1)} %bitcast.51, bf16[1,5120,384]{2,1,0:T(8,128)(2,1)S(1)} %copy-done.3), kind=kOutput, calls=%fused_computation.8 | convolution fusion | flops 3019898880 | bytes 12976128 | tf_op jit(solution)/shard_map/dot_general | solution.py:343
  201.1 15.1 %convolution_convert_fusion = bf16[768,5120]{1,0:T(8,128)(2,1)} fusion(bf16[1,384,5120]{2,1,0:T(8,128)(2,1)} %param.17, bf16[768,5120]{1,0:T(8,128)(2,1)} %bitcast.52, bf16[1,5120,384]{2,1,0:T(8,128)(2,1)} %param.16, f32[768,384]{1,0:T(8,128)} %fusion.4), kind=kOutput, calls=%fused_computation.1 | convolution fusion | flops 6045499392 | bytes 24772608 | tf_op jit(solution)/shard_map/dot_general | solution.py:346
  216.2 5.1 %all-to-all-start.1 = ((bf16[32,24,5120]{2,1,0:T(8,128)(2,1)}), bf16[32,24,5120]{2,1,0:T(8,128)(2,1)}, u32[]{:S(2)}, u32[]{:S(2)}) async-start(bf16[32,24,5120]{2,1,0:T(8,128)(2,1)} %bitcast.50), calls=%async_computation.1 | async-start | bytes 15728640 | tf_op jit(solution)/shard_map/all_to_all | solution.py:382
  221.4 2.1 copy.13
  223.5 90.4 %all-to-all-done.1 = bf16[32,24,5120]{2,1,0:T(8,128)(2,1)} async-done(((bf16[32,24,5120]{2,1,0:T(8,128)(2,1)}), bf16[32,24,5120]{2,1,0:T(8,128)(2,1)}, u32[]{:S(2)}, u32[]{:S(2)}) %all-to-all-start.1) | async-done | bytes 7864352 | tf_op jit(solution)/shard_map/all_to_all | solution.py:382
  313.9 5.2 %convert_reduce_fusion = f32[8,24,5120]{2,1,0:T(8,128)S(1)} fusion(bf16[32,24,5120]{2,1,0:T(8,128)(2,1)} %all-to-all-done.1), kind=kLoop, calls=%fused_computation | loop fusion | flops 6881280 | bytes 11796480 | tf_op jit(solution)/shard_map/reduce_sum | solution.py:394
  319.1 0.0 copy-done
  319.1 3.6 %fusion = bf16[128,5120]{1,0:T(8,128)(2,1)} fusion(f32[128,5120]{1,0:T(8,128)S(1)} %copy-done, f32[192,5120]{1,0:T(8,128)S(1)} %bitcast.48, f32[128]{0:T(128)S(1)} %bitcast.57, s32[128]{0:T(128)S(1)} %multiply_add_fusion), kind=kOutput, calls=%fused_computation.4 | convolution fusion | flops 1511309312 | bytes 7865344 | tf_op jit(solution)/shard_map/dot_general | solution.py:399
  (5 shorter events, 0.0 us)
Async XLA Ops:
  97.5 98.4 %copy-start.3 = (bf16[1,5120,384]{2,1,0:T(8,128)(2,1)S(1)}, bf16[1,5120,384]{2,1,0:T(8,128)(2,1)}, u32[]{:S(2)}) copy-start(bf16[1,5120,384]{2,1,0:T(8,128)(2,1)} %param.15) | copy-start | bytes 11796484
  192.7 3.2 copy-start.1
  216.2 97.7 %all-to-all-start.1 = ((bf16[32,24,5120]{2,1,0:T(8,128)(2,1)}), bf16[32,24,5120]{2,1,0:T(8,128)(2,1)}, u32[]{:S(2)}, u32[]{:S(2)}) async-start(bf16[32,24,5120]{2,1,0:T(8,128)(2,1)} %bitcast.50), calls=%async_computation.1 | async-start | bytes 15728640 | tf_op jit(solution)/shard_map/all_to_all | solution.py:382
  223.5 95.7 %copy-start = (f32[128,5120]{1,0:T(8,128)S(1)}, f32[128,5120]{1,0:T(8,128)}, u32[]{:S(2)}) copy-start(f32[128,5120]{1,0:T(8,128)} %copy.13) | copy-start | bytes 7864324
  223.5 95.7 %copy-start.2 = (f32[128,1]{0,1:T(1,128)S(1)}, f32[128,1]{0,1:T(1,128)}, u32[]{:S(2)}) copy-start(f32[128,1]{0,1:T(1,128)} %param.14) | copy-start | bytes 1540

commit v2 on v1

--- a/solution.py
+++ b/solution.py
@@ -53,6 +53,34 @@
         self.open.append(copy)
         return copy
 
+    def send_both(self, sources, dst, devices, core):
+        i = len(self.open)
+        copies = [
+            pltpu.make_async_remote_copy(
+                src_ref=sources[k],
+                dst_ref=dst,
+                send_sem=self.send_sems.at[i + k],
+                recv_sem=self.recv_sems.at[i + core],
+                device_id=devices[k],
+                device_id_type=MESH,
+            )
+            for k in range(2)
+        ]
+        for copy in copies:
+            copy.start()
+        self.open.extend(copies)
+        return [
+            pltpu.make_async_remote_copy(
+                src_ref=sources[k],
+                dst_ref=dst,
+                send_sem=self.send_sems.at[i + k],
+                recv_sem=self.recv_sems.at[i + k],
+                device_id=devices[k],
+                device_id_type=MESH,
+            )
+            for k in range(2)
+        ]
+
     def drain(self):
         for copy in self.open:
             copy.wait_send()
@@ -65,14 +93,18 @@
     pl.semaphore_wait(barrier, len(devices))
 
 
-A_SENDS = 96
-
-
-def project(
-    attn, w_out, resid, gain, hid_out,
+SENDS = 176
+CAP = 24
+PAIR = 2 * CAP
+ORDER = (0, 3, 1, 2)
+
+
+def layer(
+    attn, w_out, resid, gain, codes, gates, w_gate, w_up, w_down, out,
     a_buf, w_own, w0, w1, w2, res, hid,
     p_own, p0, p1, p2, l_own, l0, l1, l2, f_own, f0, f1, f2,
-    ssq, ssq_sib, send_sems, recv_sems, local_sems,
+    ssq, ssq_sib, code, gate, w_gu, w_dn, sent, rows_in, act, done, back, comb, fin,
+    send_sems, recv_sems, local_sems,
 ):
     me = Place()
     z, x, y, c = me.z, me.x, me.y, me.c
@@ -98,7 +130,29 @@
         load.start()
         load_r.append(load)
 
-    greet([sib, yp, ym, zp, zm, xp, xm])
+    loads = []
+    for half in range(2):
+        for b in range(4):
+            source = pl.ds((2 * b + half) * STRIP, STRIP)
+            target = pl.ds(b * STRIP, STRIP)
+            for k, weight in enumerate((w_gate, w_up)):
+                loads.append((weight.at[0, source], w_gu.at[half, target, pl.ds(k * 384, 384)]))
+    quarter = pl.ds(pl.multiple_of(x * 1280, 128), 1280)
+    loads.append((w_down.at[0, :, quarter], w_dn.at[pl.ds(0, 384)]))
+    loads.append((codes, code.at[0, c]))
+    loads.append((gates, gate.at[c]))
+    loads = [
+        pltpu.make_async_copy(source, target, local_sems.at[7 + k])
+        for k, (source, target) in enumerate(loads)
+    ]
+
+    def chip(dy):
+        return [(z, lax.rem(y + dy, 4) * 2 + core, x) for core in range(2)]
+
+    zo_, xs = me.at(dz=2), (None, xp, xo, xm)
+    greet([sib, *chip(1), *chip(2), *chip(3), zp, zm, zo_, xp, xm, xo])
+    for load in loads:
+        load.start()
 
     def rows_q(half=None):
         start = z * QN
@@ -138,6 +192,18 @@
             links.send(resid.at[:, pl.ds(col, STRIP)], res.at[c, :, pl.ds(b * STRIP, STRIP)], sib)
         )
 
+    sib_code = links.send(codes, code.at[0, c], sib)
+    sib_gate = links.send(gates, gate.at[c], sib)
+    dn_rows = pl.multiple_of(z * 96, 16)
+    dn_x = {}
+    for dx in (1, 3, 2):
+        column = pl.multiple_of(lax.rem(x + dx, 4) * 1280, 128)
+        dn_x[4 - dx] = links.send(
+            w_down.at[0, pl.ds(dn_rows, 96), pl.ds(column, 1280)],
+            w_dn.at[pl.ds((4 - dx) * 384 + dn_rows, 96)],
+            xs[dx],
+        )
+
     def multiply(block, part, core, col, width):
         def step(m, carry):
             rows = pl.ds(pl.multiple_of(m * 256, 256), 256)
@@ -237,6 +303,9 @@
     sib_a.wait_recv()
     multiply(w_own, p_own, 1 - c, 0, STRIP)
     first["own"] = reduce_first(p_own, l_own, f_own)
+    loads[-2].wait()
+    sib_code.wait_recv()
+    code_x = {4 - dx: links.send(code.at[0], code.at[4 - dx], xs[dx]) for dx in (1, 3, 2)}
     on_q(0)
     second["own"] = reduce_second(first["own"], p_own, l_own, f_own)
 
@@ -280,6 +349,12 @@
             finish("own", p_own, f_own, [(pl.multiple_of(y * STRIP, 128), 0)], STRIP)
         else:
             second[j - 1] = reduce_second(first[j - 1], parts[j - 1], relays[j - 1], finals[j - 1])
+        if j == n - 1:
+            dn_z = []
+            for slot in (3, 1, 2):
+                dn_x[slot].wait_recv()
+                piece = w_dn.at[pl.ds(slot * 384 + dn_rows, 96)]
+                dn_z.extend(links.send(piece, piece, device) for device in (zp, zm, zo_))
         all_in(j)
         first[j] = compute(j)
         if j + 1 < n:
@@ -290,15 +365,179 @@
     second[last] = reduce_second(first[last], parts[last], relays[last], finals[last])
     finish(last, parts[last], finals[last], strips_of(last), WIDTHS[last])
 
-    back = links.send(hid.at[1 - c], hid_out.at[c], sib)
-    keep = pltpu.make_async_copy(hid.at[c], hid_out.at[c], local_sems.at[6])
-    keep.start()
-    back.wait_recv()
-    keep.wait()
+    share = links.send(ssq, ssq_sib, sib)
+
+    def pick(slot, chips):
+        blocks = []
+        for dy in chips:
+            base = lax.rem(y + dy, 4) * (2 * PAIR)
+            place = base + lax.broadcasted_iota(jnp.int32, (2 * PAIR, 128), 0)
+            blocks.append(
+                jnp.concatenate(
+                    [
+                        (place == code[slot, core, 0:1, :]).astype(F32).astype(BF)
+                        for core in range(2)
+                    ],
+                    axis=1,
+                )
+            )
+        return blocks[0] if len(blocks) == 1 else jnp.concatenate(blocks, axis=0)
+
+    loads[-1].wait()
+    sib_gate.wait_recv()
+    share.wait_recv()
+    for core in range(2):
+        scale = lax.rsqrt((ssq[core] + ssq_sib[core])[:, 0:1] / 5120.0 + 1e-06)
+        for b in range(4):
+            cols = pl.ds(b * STRIP, STRIP)
+            col = pl.multiple_of((2 * b + c) * STRIP, 128)
+            res[core, :, cols] = (hid[core, :, cols] * scale * gain[0:1, pl.ds(col, STRIP)]).astype(BF)
+
+    arrive = {}
+
+    def dispatch(dy):
+        choice = pick(0, (dy,))
+        for b in range(4):
+            cols = pl.ds(b * STRIP, STRIP)
+            normed = res[:, :, cols].reshape(256, STRIP)
+            rows = jnp.dot(choice, normed, preferred_element_type=F32).astype(BF)
+            sent[dy, :, :, cols] = rows.reshape(2, PAIR, STRIP)
+        slot = (4 - dy) % 4
+        if dy == 0:
+            arrive[0] = [links.send(sent.at[0, 1 - c], rows_in.at[0, 0, c], sib)]
+            rows_in[0, 0, c] = sent[0, c]
+        else:
+            arrive[slot] = links.send_both(
+                [sent.at[dy, 0], sent.at[dy, 1]], rows_in.at[slot, 0, c], chip(dy), c
+            )
+
+    spread, relay_x = {}, {}
+
+    def spread_rows(r):
+        for copy in arrive[r]:
+            copy.wait_recv()
+        spread[r] = (
+            links.send(rows_in.at[r, 0], rows_in.at[r, 3], xp),
+            links.send(rows_in.at[r, 0], rows_in.at[r, 1], xm),
+        )
+
+    def relay_rows(r):
+        spread[r][0].wait_recv()
+        one = links.send(rows_in.at[r, 3, 0], rows_in.at[r, 2, 0], xp)
+        spread[r][1].wait_recv()
+        two = links.send(rows_in.at[r, 1, 1], rows_in.at[r, 2, 1], xm)
+        relay_x[r] = (one, two)
+
+    act_x = {}
+
+    def gate_up(r):
+        for copy in relay_x[r]:
+            copy.wait_recv()
+        both = jnp.dot(
+            rows_in[r, :, 0].reshape(4 * PAIR, 4 * STRIP), w_gu[0], preferred_element_type=F32
+        ) + jnp.dot(
+            rows_in[r, :, 1].reshape(4 * PAIR, 4 * STRIP), w_gu[1], preferred_element_type=F32
+        )
+        left, right = both[:, :384], both[:, 384:]
+        made = (left / (1.0 + jnp.exp(-left)) * right).astype(BF).reshape(4, PAIR, 384)
+        for slot in range(4):
+            act[r, lax.rem(x + slot, 4), :, pl.ds(0, 384)] = made[slot]
+        mine = act.at[r, :, :, pl.ds(0, 384)]
+        act_x[r] = [
+            links.send(mine, act.at[r, :, :, pl.ds((4 - dx) * 384, 384)], xs[dx]) for dx in (2, 1, 3)
+        ]
+
+    home = {}
+
+    def down(r, final):
+        for copy in act_x[r]:
+            copy.wait_recv()
+        whole = jnp.dot(
+            act[r].reshape(4 * PAIR, 1536), w_dn[...], preferred_element_type=F32
+        ).astype(BF).reshape(4, PAIR, 1280)
+        for core in range(2):
+            done[r, core] = whole[:, :, core * STRIP:(core + 1) * STRIP]
+        slot = (4 - r) % 4
+        if r == 0:
+            home[0] = [links.send(done.at[0, 1 - c], back.at[0, c], sib)]
+            back[0, c] = done[0, c]
+        elif not final:
+            home[slot] = links.send_both([done.at[r, 0], done.at[r, 1]], back.at[slot, c], chip(r), c)
+        else:
+            home[slot] = []
+            for dx in (2, 1, 3, 0):
+                t = lax.rem(x + dx, 4)
+                home[slot].append(
+                    links.send_both(
+                        [done.at[r, 0, t], done.at[r, 1, t]], back.at[slot, c, t], chip(r), c
+                    )
+                )
+
+    for dy in (0, 1, 3, 2):
+        dispatch(dy)
+        if dy == 0:
+            spread_rows(0)
+    for load in loads[:-2]:
+        load.wait()
+    for slot in (1, 2, 3):
+        code_x[slot].wait_recv()
+    spread_rows(ORDER[1])
+    for k, r in enumerate(ORDER):
+        relay_rows(r)
+        if k + 2 < 4:
+            spread_rows(ORDER[k + 2])
+        gate_up(r)
+        if k == 1:
+            for copy in dn_z:
+                copy.wait_recv()
+        if k > 0:
+            down(ORDER[k - 1], False)
+    down(ORDER[3], True)
+
+    ending = (4 - ORDER[3]) % 4
+    for slot in range(4):
+        if slot != ending:
+            for copy in home[slot]:
+                copy.wait_recv()
+    over_x = {}
+    for k, dx in enumerate((2, 1, 3, 0)):
+        for copy in home[ending][k]:
+            copy.wait_recv()
+        t = lax.rem(x + dx, 4)
+        mixed = lax.dot_general(
+            pick(dx, (0, 1, 2, 3)),
+            back[:, :, t].reshape(8 * PAIR, STRIP),
+            (((0,), (0,)), ((), ())),
+            preferred_element_type=F32,
+        ).astype(BF)
+        if dx == 0:
+            fin[0] = mixed
+        else:
+            comb[dx] = mixed
+            over_x[4 - dx] = links.send(comb.at[dx], fin.at[4 - dx], xs[dx])
+
+    leave, stay = [], []
+    for slot in (0, 1, 3, 2):
+        if slot:
+            over_x[slot].wait_recv()
+        b = lax.rem(x + slot, 4)
+        cols = pl.ds(pl.multiple_of(b * STRIP, 128), STRIP)
+        col = pl.ds(pl.multiple_of((2 * b + c) * STRIP, 128), STRIP)
+        for core in range(2):
+            rows = fin[slot, pl.ds(core * 128, 128), :].astype(F32)
+            res[core, :, cols] = (hid[core, :, cols] + gate[core][:, 0:1] * rows).astype(BF)
+        leave.append(links.send(res.at[1 - c, :, cols], out.at[:, col], sib))
+        keep = pltpu.make_async_copy(res.at[c, :, cols], out.at[:, col], local_sems.at[2 + slot])
+        keep.start()
+        stay.append(keep)
+    for copy in leave:
+        copy.wait_recv()
+    for copy in stay:
+        copy.wait()
     links.drain()
 
 
-def scratch_a():
+def scratch():
     def triple(shape):
         return [pltpu.VMEM(shape(STRIP), BF)] + [pltpu.VMEM(shape(3 * v), BF) for v in WIDTHS]
 
@@ -313,9 +552,20 @@
         *triple(lambda v: (2, 2, 128, v)),
         pltpu.VMEM((2, 128, 128), F32),
         pltpu.VMEM((2, 128, 128), F32),
-        pltpu.SemaphoreType.DMA((A_SENDS,)),
-        pltpu.SemaphoreType.DMA((A_SENDS,)),
-        pltpu.SemaphoreType.DMA((8,)),
+        pltpu.VMEM((4, 2, 8, 128), jnp.int32),
+        pltpu.VMEM((2, 128, 128), F32),
+        pltpu.VMEM((2, 4 * STRIP, 768), BF),
+        pltpu.VMEM((1536, 1280), BF),
+        pltpu.VMEM((4, 2, PAIR, 4 * STRIP), BF),
+        pltpu.VMEM((4, 4, 2, PAIR, 4 * STRIP), BF),
+        pltpu.VMEM((4, 4, PAIR, 1536), BF),
+        pltpu.VMEM((4, 2, 4, PAIR, STRIP), BF),
+        pltpu.VMEM((4, 2, 4, PAIR, STRIP), BF),
+        pltpu.VMEM((4, 256, STRIP), BF),
+        pltpu.VMEM((4, 256, STRIP), BF),
+        pltpu.SemaphoreType.DMA((SENDS,)),
+        pltpu.SemaphoreType.DMA((SENDS,)),
+        pltpu.SemaphoreType.DMA((32,)),
     ]
 
 
@@ -323,86 +573,33 @@
 VM = pl.BlockSpec(memory_space=pltpu.VMEM)
 
 
-def call_a(attn, w_out, resid, gain):
+def shards(attn, w_out, resid, norm_gain, route_ids, gate_vals, w_gate, w_up, w_down):
+    core = lax.axis_index("expert") % 2
+    ids = route_ids.reshape(-1)
+    one_hot = (ids[:, None] == jnp.arange(8, dtype=jnp.int32)[None, :]).astype(jnp.int32)
+    earlier = jnp.cumsum(one_hot, axis=0) - one_hot
+    code = ids * PAIR + core * CAP + jnp.sum(earlier * one_hot, axis=1)
     return pl.pallas_call(
-        project,
-        out_shape=jax.ShapeDtypeStruct((2, 128, 4 * STRIP), F32),
-        in_specs=[ANY, ANY, ANY, VM],
+        layer,
+        out_shape=jax.ShapeDtypeStruct(resid.shape, BF),
+        in_specs=[ANY, ANY, ANY, VM, ANY, ANY, ANY, ANY, ANY],
         out_specs=ANY,
-        scratch_shapes=scratch_a(),
+        scratch_shapes=scratch(),
         compiler_params=pltpu.CompilerParams(
-            collective_id=0, has_side_effects=True, vmem_limit_bytes=56 * 2**20
+            collective_id=0, has_side_effects=True, vmem_limit_bytes=62 * 2**20
         ),
-        name="project",
-    )(attn, w_out, resid, gain)
-
-
-def expert_rows(received, w_gate, w_up, w_down):
-    layout = received.shape
-    flat_rows = received.reshape(-1, layout[-1])
-    gate_act = jnp.dot(flat_rows, w_gate[0], preferred_element_type=F32)
-    up_act = jnp.dot(flat_rows, w_up[0], preferred_element_type=F32)
-    activation = (jax.nn.silu(gate_act) * up_act).astype(BF)
-    down_part = jnp.dot(activation, w_down[0], preferred_element_type=F32).astype(BF)
-    return down_part.reshape(layout)
-
-
-def shards(attn, w_out, resid, norm_gain, route_ids, gate_vals, w_gate, w_up, w_down):
-    row_count = resid.shape[0]
-    width_model = resid.shape[1]
-    top_count = route_ids.shape[1]
-    expert_count = lax.axis_size("expert")
-    group_width = lax.axis_size("tensor")
-    capacity = min(row_count, 3 * row_count * top_count // (2 * expert_count))
-    halves = call_a(attn, w_out, resid, norm_gain.reshape(1, -1))
-    hidden = halves.reshape(2, 128, 4, STRIP).transpose(1, 2, 0, 3).reshape(128, width_model)
-    scale_inv = lax.rsqrt(jnp.mean(hidden * hidden, axis=1, keepdims=True) + 1e-06)
-    normed = (hidden * scale_inv * norm_gain).astype(jnp.bfloat16)
-    pair_ids = route_ids.reshape(-1)
-    one_hot = (pair_ids[:, None] == jnp.arange(expert_count, dtype=jnp.int32)[None, :]).astype(
-        jnp.int32
+        name="layer",
+    )(
+        attn,
+        w_out,
+        resid,
+        norm_gain.reshape(1, -1),
+        jnp.broadcast_to(code[None, :], (8, 128)),
+        jnp.broadcast_to(gate_vals, (128, 128)),
+        w_gate,
+        w_up,
+        w_down,
     )
-    earlier = jnp.cumsum(one_hot, axis=0) - one_hot
-    slot_index = jnp.sum(earlier * one_hot, axis=1)
-    target = pair_ids * capacity + slot_index
-    placed = (
-        jnp.arange(expert_count * capacity, dtype=jnp.int32)[:, None] == target[None, :]
-    ).astype(jnp.float32)
-    placed_rows = placed.reshape(expert_count * capacity, row_count, top_count)
-    dispatch = jnp.sum(placed_rows, axis=2)
-    weights_comb = jnp.sum(placed_rows * gate_vals[None, :, :], axis=2)
-    send_rows = jnp.dot(
-        dispatch.astype(jnp.bfloat16), normed, preferred_element_type=jnp.float32
-    ).astype(jnp.bfloat16)
-    send_rows = send_rows.reshape(expert_count, capacity, width_model)
-    copies = jnp.broadcast_to(
-        send_rows[:, None], (expert_count, group_width, capacity, width_model)
-    )
-    copies = copies.reshape(expert_count * group_width, capacity, width_model)
-    returned = lax.all_to_all(
-        expert_rows(
-            lax.all_to_all(copies, ("expert", "tensor"), split_axis=0, concat_axis=0, tiled=True),
-            w_gate,
-            w_up,
-            w_down,
-        ),
-        ("expert", "tensor"),
-        split_axis=0,
-        concat_axis=0,
-        tiled=True,
-    )
-    quarters = jnp.sum(
-        returned.reshape(expert_count, group_width, capacity, width_model),
-        axis=1,
-        dtype=jnp.float32,
-    )
-    mixture = jnp.dot(
-        weights_comb.T,
-        quarters.reshape(expert_count * capacity, width_model),
-        precision=lax.Precision.HIGHEST,
-        preferred_element_type=jnp.float32,
-    )
-    return (hidden + mixture).astype(jnp.bfloat16)
 
 
 def solution(mesh):

time: 325 us -> 218 us (0.67)
  Pallas kernels: 83.8 us -> 211 us
  blocking collectives: 95.2 us -> 0 us
  waiting for transfers between devices: 90.4 us -> 0 us
  matrix products: 24.7 us -> 0 us
  local copies, waits for them, and re-layouts: 14.1 us -> 4.42 us
  other arithmetic: 9.33 us -> 2.4 us
  starting transfers between devices: 5.13 us -> 0 us
    pallas_call x1, Pallas kernels: 83.8 us -> 211 us  [shards(): pl.pallas_call(layer, out_shape=jax.ShapeDtypeStruct(resid.shape, BF), in...]
    all_to_all x1 -> x0, blocking collectives: 95.2 us -> none  [shards(): lax.all_to_all(copies, ('expert', 'tensor'), split_axis=0, concat_axis=0,...]
    all_to_all x1 -> x0, waiting for transfers between devices: 90.4 us -> none  [shards(): lax.all_to_all(expert_rows(lax.all_to_all(copies, ('expert', 'tensor'), s...]
    dot_general x4 -> x0, matrix products: 24.7 us -> none  [the longest x1 15.1 us: expert_rows(): jnp.dot(activation, w_down[0], preferred_element_type=F32).astype(BF)]
    reshape x3 -> x0, local copies, waits for them, and re-layouts: 9.2 us -> none  [shards(): halves.reshape(2, 128, 4, STRIP).transpose(1, 2, 0, 3)]
    reduce_sum x3 -> x1, other arithmetic: 6.73 us -> 0.83 us  [shards(): code = ids * PAIR + core * CAP + jnp.sum(earlier * one_hot, axis=1)]
    all_to_all x1 -> x0, starting transfers between devices: 5.13 us -> none  [shards(): lax.all_to_all(expert_rows(lax.all_to_all(copies, ('expert', 'tensor'), s...]
  transfers between devices with their start and end apart: 1 -> 0, of which waited for: 1 -> 0; matrix products, arithmetic and copies ran while one was open for 1% -> 0% of each run, Pallas kernels for 0% -> 0%
where the time goes in v2:
time: 218 us
  Pallas kernels  211 us (97%)
  local copies, waits for them, and re-layouts  4.42 us (2%)
  other arithmetic  2.4 us (1%)
    pallas_call x1, Pallas kernels, shards(): pl.pallas_call(layer, out_shape=jax.ShapeDtypeStruct(resid.shape, BF), in...  211 us

profile of v2, /device:TPU:1, one launch (start us, length us, event | category | flops | bytes accessed | tf_op | source)
XLA Modules:
  0.0 218.2 jit_solution(106345090087384087)
XLA Ops:
  0.0 1.4 broadcast_in_dim.16.gates
  1.4 0.7 fusion
  2.1 0.2 reduce_window_sum.11
  2.3 0.8 select_reduce_fusion
  3.1 0.7 add_add_fusion
  3.8 0.6 broadcast_in_dim.6.codes
  4.4 211.4 %layer.1 = bf16[128,5120]{1,0:T(8,128)(2,1)} custom-call(bf16[512,2048]{1,0:T(8,128)(2,1)} %attn.1, bf16[2048,640]{1,0:T(8,128)(2,1)} %w_out.1, bf16[128,5120]{1,0:T(8,128)(2,1)} %resid.1, f32[1,5120]{1,0:T(1,128)} %bitcast.4, s32[8,128]{1,0:T(8,128)} %broadcast_in_dim.6.codes, f32[128,128]{1,0:T(8,128)} %broadcast_in_dim.16.gates, ...), custom_call_target="tpu_custom_call" | custom-call | tf_op jit(solution)/shard_map/layer/pallas_call | solution.py:582
  215.8 2.5 %copy.11 = bf16[128,5120]{1,0:T(8,128)(2,1)} copy(bf16[128,5120]{1,0:T(8,128)(2,1)} %layer.1) | data formatting | bytes 2621440

commit v3 on v2

v3 whole, which is shorter than its diff:
```python
import functools

import jax
import jax.numpy as jnp
from jax import lax
from jax.experimental import pallas as pl
from jax.experimental.pallas import tpu as pltpu
from jax.sharding import PartitionSpec as P

MESH = pl.DeviceIdType.MESH
BF = jnp.bfloat16
F32 = jnp.float32

QN = 336
DN = 2048 - 4 * QN
QH = 176
PIECES = 5
WIDE = 128
STRIP = 640


class Place:
    def __init__(self):
        self.z = lax.axis_index("dp")
        self.e = lax.axis_index("expert")
        self.x = lax.axis_index("tensor")
        self.y = self.e // 2
        self.c = self.e % 2

    def at(self, dx=0, dy=0, dz=0, flip=False):
        core = 1 - self.c if flip else self.c
        return (
            lax.rem(self.z + dz, 4),
            lax.rem(self.y + dy, 4) * 2 + core,
            lax.rem(self.x + dx, 4),
        )


class Links:
    def __init__(self, send_sems, recv_sems):
        self.send_sems, self.recv_sems, self.open = send_sems, recv_sems, []

    def send(self, src, dst, device):
        i = len(self.open)
        copy = pltpu.make_async_remote_copy(
            src_ref=src,
            dst_ref=dst,
            send_sem=self.send_sems.at[i],
            recv_sem=self.recv_sems.at[i],
            device_id=device,
            device_id_type=MESH,
        )
        copy.start()
        self.open.append(copy)
        return copy

    def send_both(self, sources, dst, devices, core):
        i = len(self.open)
        copies = [
            pltpu.make_async_remote_copy(
                src_ref=sources[k],
                dst_ref=dst,
                send_sem=self.send_sems.at[i + k],
                recv_sem=self.recv_sems.at[i + core],
                device_id=devices[k],
                device_id_type=MESH,
            )
            for k in range(2)
        ]
        for copy in copies:
            copy.start()
        self.open.extend(copies)
        return [
            pltpu.make_async_remote_copy(
                src_ref=sources[k],
                dst_ref=dst,
                send_sem=self.send_sems.at[i + k],
                recv_sem=self.recv_sems.at[i + k],
                device_id=devices[k],
                device_id_type=MESH,
            )
            for k in range(2)
        ]

    def drain(self):
        for copy in self.open:
            copy.wait_send()


def greet(devices):
    barrier = pltpu.get_barrier_semaphore()
    for device in devices:
        pl.semaphore_signal(barrier, inc=1, device_id=device, device_id_type=MESH)
    pl.semaphore_wait(barrier, len(devices))


SENDS = 256
CAP = 24
PAIR = 2 * CAP
LAST = 3
PLAN = (
    "sq1", "siba", "sq0", "sd0", "wdx", "onq1", "onq0", "ownc", "sd1", "sq4", "sq3", "onz1", "owns",
    "rs1own", "onrq0", "ond0", "onrq1", "onz0", "onzo0", "onq4", "ond1", "sd4", "rs2own", "onzo1", "sq2",
    "across0", "onrq4", "onq3", "sides0", "rs10", "onz4", "sides1", "ond4", "across1", "sd3", "rs20",
    "onzo4", "onrq3", "onz3", "rs11", "code", "sd2", "sides4", "onq2", "across4", "rs14", "ond3", "onzo3",
    "sides3", "finown", "rs21", "onrq2", "rs24", "ond2", "across3", "fin0", "rs13", "onzo2", "onz2",
    "across2", "rs23", "sides2", "rs12", "fin1", "rs22", "fin4", "fin3", "fin2", "share", "codex", "norm",
    "disp0", "disp2", "spread0", "other", "disp3", "spread2", "disp1", "spread3", "wdz", "relay2", "spread1",
    "gu2", "act2", "relay1", "relay0", "ract2", "gu1", "act1", "wdw", "relay3", "down2", "gu0", "ract1",
    "act0", "gu3", "act3", "down1", "ract0", "down3", "down0", "homes", "comb2", "comb3", "comb1", "comb0",
    "out0", "out2", "out1", "out3",
)


def layer(
    attn, w_out, resid, gain, ids, gates, w_gate, w_up, w_down, out,
    a_buf, w_own, w, res, hid, hid_sib, p_own, parts, l_own, relays, f_own, finals,
    ssq, ssq_sib, code, w_gu, w_dn, sent, rows_in, act, done, back, comb, fin,
    send_sems, recv_sems, local_sems,
):
    me = Place()
    z, x, y, c = me.z, me.x, me.y, me.c
    sib = me.at(flip=True)
    xp, xm, xo = me.at(dx=1), me.at(dx=3), me.at(dx=2)
    yp, ym, zp, zm = me.at(dy=1), me.at(dy=3), me.at(dz=1), me.at(dz=3)
    links = Links(send_sems, recv_sems)

    load_w = [
        pltpu.make_async_copy(w_out.at[:, pl.ds(j * WIDE, WIDE)], w_own.at[j], local_sems.at[30 + j])
        for j in range(PIECES)
    ]
    for load in load_w:
        load.start()
    load_a = pltpu.make_async_copy(attn, a_buf.at[c], local_sems.at[1])
    load_a.start()
    load_r = []
    for b in range(4):
        col = pl.multiple_of((2 * b + c) * STRIP, 128)
        load = pltpu.make_async_copy(
            resid.at[:, pl.ds(col, STRIP)], res.at[c, :, pl.ds(b * STRIP, STRIP)], local_sems.at[2 + b]
        )
        load.start()
        load_r.append(load)

    loads = []
    for half in range(2):
        for b in range(4):
            source = pl.ds((2 * b + half) * STRIP, STRIP)
            target = pl.ds(b * STRIP, STRIP)
            for k, weight in enumerate((w_gate, w_up)):
                loads.append((weight.at[0, source], w_gu.at[half, target, pl.ds(k * 384, 384)]))
    quarter = pl.ds(pl.multiple_of(x * 1280, 128), 1280)
    loads.append((w_down.at[0, :, quarter], w_dn.at[pl.ds(0, 384)]))
    loads = [
        pltpu.make_async_copy(source, target, local_sems.at[7 + k])
        for k, (source, target) in enumerate(loads)
    ]

    def chip(dy, dx=0):
        return [(z, lax.rem(y + dy, 4) * 2 + core, lax.rem(x + dx, 4)) for core in range(2)]

    zo_, xs = me.at(dz=2), (None, xp, xo, xm)
    greet([sib, *chip(1), *chip(2), *chip(3), zp, zm, zo_, *chip(0, 1), *chip(0, 2), *chip(0, 3)])
    for load in loads:
        load.start()

    def rows_q(half=None):
        start = z * QN
        if half is None:
            return pl.ds(pl.multiple_of(start, 16), QN)
        return pl.ds(pl.multiple_of(start + half * QH, 16), QN - QH if half else QH)

    rows_d = pl.ds(4 * QN, DN)

    def rows_dh(half):
        return pl.ds(4 * QN + half * (DN // 2), DN // 2)

    def own(j, rows):
        return w_own.at[j, rows]

    def send_q(j):
        return (
            links.send(own(j, rows_q()), w.at[j, 1, rows_q()], yp),
            links.send(own(j, rows_q()), w.at[j, 0, rows_q()], ym),
        )

    def send_d(j):
        return (
            links.send(own(j, rows_d), w.at[j, 1, rows_d], yp),
            links.send(own(j, rows_d), w.at[j, 0, rows_d], ym),
        )

    n = PIECES
    q, d, rq, rd, zs, zo, zr, side, first, second = ({} for _ in range(10))
    steps = {}

    def step(name, run, *args):
        steps[name] = functools.partial(run, *args)

    loaded = set()

    def need(j):
        if j not in loaded:
            load_w[j].wait()
            loaded.add(j)

    def start_q(j):
        need(j)
        q[j] = send_q(j)

    def start_d(j):
        need(j)
        d[j] = send_d(j)

    def start_sibling():
        side["attn"] = links.send(attn, a_buf.at[c], sib)
        side["resid"] = []
        for b in range(4):
            col = pl.multiple_of((2 * b + 1 - c) * STRIP, 128)
            side["resid"].append(
                links.send(resid.at[:, pl.ds(col, STRIP)], res.at[c, :, pl.ds(b * STRIP, STRIP)], sib)
            )

    dn_rows = pl.multiple_of(z * 96, 16)
    dn_x, dn_z = {}, []

    def start_dn():
        for dx in (1, 3, 2):
            column = pl.multiple_of(lax.rem(x + dx, 4) * 1280, 128)
            dn_x[4 - dx] = links.send(
                w_down.at[0, pl.ds(dn_rows, 96), pl.ds(column, 1280)],
                w_dn.at[pl.ds((4 - dx) * 384 + dn_rows, 96)],
                xs[dx],
            )

    def share_dn():
        for slot in (3, 1, 2):
            dn_x[slot].wait_recv()
            piece = w_dn.at[pl.ds(slot * 384 + dn_rows, 96)]
            dn_z.extend(links.send(piece, piece, device) for device in (zp, zm, zo_))

    def wait_dn():
        for copy in dn_z:
            copy.wait_recv()

    def multiply(blocks, part, core, col):
        def step(m, carry):
            rows = pl.ds(pl.multiple_of(m * 256, 256), 256)
            right = blocks[0][...]
            if len(blocks) > 1:
                right = jnp.concatenate([block[...] for block in blocks], axis=1)
            result = jnp.dot(a_buf[core, rows, :], right, preferred_element_type=F32).astype(BF)
            cols = pl.ds(col, right.shape[1])
            part[2 * m, core, :, cols] = result[:128]
            part[2 * m + 1, core, :, cols] = result[128:]
            return carry

        lax.fori_loop(0, 2, step, 0)

    ahead, behind, over = lax.rem(x + 1, 4), lax.rem(x + 3, 4), lax.rem(x + 2, 4)

    def reduce_first(part, relay, final):
        return (
            links.send(part.at[over, 0], relay.at[0], xp),
            links.send(part.at[over, 1], relay.at[1], xm),
            links.send(part.at[ahead, 1], final.at[0, 1], xp),
            links.send(part.at[behind, 0], final.at[1, 0], xm),
        )

    def reduce_second(first, part, relay, final):
        first[0].wait_recv()
        part[ahead, 0] = (part[ahead, 0].astype(F32) + relay[0].astype(F32)).astype(BF)
        one = links.send(part.at[ahead, 0], final.at[0, 0], xp)
        first[1].wait_recv()
        part[behind, 1] = (part[behind, 1].astype(F32) + relay[1].astype(F32)).astype(BF)
        two = links.send(part.at[behind, 1], final.at[1, 1], xm)
        return (first[2], first[3], one, two)

    def on_q(j):
        q[j][0].wait_recv()
        one = links.send(w.at[j, 1, rows_q(0)], w.at[j, 2, rows_q(0)], yp)
        z_a = (
            links.send(w.at[j, 1, rows_q()], w.at[j, 1, rows_q()], zp),
            links.send(w.at[j, 1, rows_q()], w.at[j, 1, rows_q()], zm),
        )
        q[j][1].wait_recv()
        two = links.send(w.at[j, 0, rows_q(1)], w.at[j, 2, rows_q(1)], ym)
        z_b = (
            links.send(w.at[j, 0, rows_q()], w.at[j, 0, rows_q()], zp),
            links.send(w.at[j, 0, rows_q()], w.at[j, 0, rows_q()], zm),
        )
        rq[j] = (one, two)
        zs[j] = (z_a, z_b)

    def on_rq(j):
        rq[j][0].wait_recv()
        rq[j][1].wait_recv()
        zo[j] = (
            links.send(w.at[j, 2, rows_q()], w.at[j, 2, rows_q()], zp),
            links.send(w.at[j, 2, rows_q()], w.at[j, 2, rows_q()], zm),
        )

    def on_d(j):
        d[j][0].wait_recv()
        one = links.send(w.at[j, 1, rows_dh(0)], w.at[j, 2, rows_dh(0)], yp)
        d[j][1].wait_recv()
        two = links.send(w.at[j, 0, rows_dh(1)], w.at[j, 2, rows_dh(1)], ym)
        rd[j] = (one, two)

    def z_relay(j, pair, slot):
        low = pl.ds(pl.multiple_of(lax.rem(z + 3, 4) * QN, 16), QH)
        high = pl.ds(pl.multiple_of(lax.rem(z + 1, 4) * QN + QH, 16), QN - QH)
        pair[0].wait_recv()
        one = links.send(w.at[j, slot, low], w.at[j, slot, low], zp)
        pair[1].wait_recv()
        two = links.send(w.at[j, slot, high], w.at[j, slot, high], zm)
        zr[j, slot] = (one, two)

    def on_z(j):
        z_relay(j, zs[j][0], 1)
        z_relay(j, zs[j][1], 0)

    def on_zo(j):
        z_relay(j, zo[j], 2)

    def sides(j):
        for copy in (*zr[j, 0], *zr[j, 1]):
            copy.wait_recv()
        for core in range(2):
            multiply([w.at[j, 0], w.at[j, 1]], parts.at[j], core, 0)

    def across(j):
        for copy in (*rd[j], *zr[j, 2]):
            copy.wait_recv()
        for core in range(2):
            multiply([w.at[j, 2]], parts.at[j], core, 2 * WIDE)

    def group(j):
        return (p_own, l_own, f_own) if j == "own" else (parts.at[j], relays.at[j], finals.at[j])

    def first_half(j):
        first[j] = reduce_first(*group(j))

    def second_half(j):
        second[j] = reduce_second(first[j], *group(j))

    own_pieces = [w_own.at[j] for j in range(PIECES)]

    def own_tokens():
        load_a.wait()
        for j in range(n):
            need(j)
        multiply(own_pieces, p_own, c, 0)

    def sibling_tokens():
        side["attn"].wait_recv()
        multiply(own_pieces, p_own, 1 - c, 0)

    def place_tokens():
        experts = lax.broadcasted_iota(jnp.int32, (8, 128), 0)
        named = ids[...] == experts
        counts = named.astype(F32)
        before = lax.broadcasted_iota(jnp.int32, (128, 128), 0) < lax.broadcasted_iota(
            jnp.int32, (128, 128), 1
        )
        earlier = jnp.dot(counts.astype(BF), before.astype(F32).astype(BF), preferred_element_type=F32)
        slots = jnp.sum(jnp.where(named, earlier, 0.0), axis=0, keepdims=True).astype(jnp.int32)
        code[0, c] = jnp.broadcast_to(ids[...] * PAIR + c * CAP + slots, (8, 128))
        side["code"] = links.send(code.at[0, c], code.at[0, c], sib)

    def share_code():
        side["code"].wait_recv()
        side["codes"] = [links.send(code.at[0], code.at[4 - dx], xs[dx]) for dx in (1, 3, 2)]

    def finish(group, part, final, strips, width):
        for copy in second[group]:
            copy.wait_recv()
        for k, (col, strip) in enumerate(strips):
            cols = pl.ds(col, width)
            for core in range(2):
                at = pl.ds(k * width, width)
                total = (
                    res[core, :, cols].astype(F32)
                    + part[x, core, :, at].astype(F32)
                    + final[0, core, :, at].astype(F32)
                    + final[1, core, :, at].astype(F32)
                )
                hid[core, :, cols] = total
                add = jnp.sum(total * total, axis=1, keepdims=True)
                ssq[core] = ssq[core] + jnp.broadcast_to(add, (128, 128))

    ssq[...] = jnp.zeros_like(ssq)

    def finish_piece(j):
        strips = [
            (pl.multiple_of(lax.rem(y + dy, 4) * STRIP + j * WIDE, 128), k)
            for k, dy in enumerate((1, 3, 2))
        ]
        finish(j, parts.at[j], finals.at[j], strips, WIDE)

    def finish_own():
        for load in load_r:
            load.wait()
        for copy in side["resid"]:
            copy.wait_recv()
        finish("own", p_own, f_own, [(pl.multiple_of(y * STRIP, 128), 0)], STRIP)

    def start_share():
        side["ssq"] = links.send(ssq, ssq_sib, sib)

    def start_other():
        side["hid"] = links.send(hid.at[1 - c], hid_sib, sib)


    def pick(slot, chips):
        blocks = []
        for dy in chips:
            base = lax.rem(y + dy, 4) * (2 * PAIR)
            place = base + lax.broadcasted_iota(jnp.int32, (2 * PAIR, 128), 0)
            blocks.append(
                jnp.concatenate(
                    [
                        (place == code[slot, core, 0:1, :]).astype(F32).astype(BF)
                        for core in range(2)
                    ],
                    axis=1,
                )
            )
        return blocks[0] if len(blocks) == 1 else jnp.concatenate(blocks, axis=0)

    def normalize():
        side["ssq"].wait_recv()
        for core in range(2):
            scale = lax.rsqrt((ssq[core] + ssq_sib[core])[:, 0:1] / 5120.0 + 1e-06)
            for b in range(4):
                cols = pl.ds(b * STRIP, STRIP)
                col = pl.multiple_of((2 * b + c) * STRIP, 128)
                res[core, :, cols] = (hid[core, :, cols] * scale * gain[0:1, pl.ds(col, STRIP)]).astype(BF)
        for load in loads:
            load.wait()

    arrive = {}

    def dispatch(r):
        dy = (4 - r) % 4
        choice = pick(0, (dy,))
        for b in range(4):
            cols = pl.ds(b * STRIP, STRIP)
            normed = res[:, :, cols].reshape(256, STRIP)
            rows = jnp.dot(choice, normed, preferred_element_type=F32).astype(BF)
            sent[dy, :, :, cols] = rows.reshape(2, PAIR, STRIP)
        slot = (4 - dy) % 4
        if dy == 0:
            arrive[0] = [links.send(sent.at[0, 1 - c], rows_in.at[0, 0, c], sib)]
            rows_in[0, 0, c] = sent[0, c]
        else:
            arrive[slot] = links.send_both(
                [sent.at[dy, 0], sent.at[dy, 1]], rows_in.at[slot, 0, c], chip(dy), c
            )

    spread, relay_x = {}, {}

    def spread_rows(r):
        for copy in arrive[r]:
            copy.wait_recv()
        spread[r] = (
            links.send(rows_in.at[r, 0], rows_in.at[r, 3], xp),
            links.send(rows_in.at[r, 0], rows_in.at[r, 1], xm),
        )

    def relay_rows(r):
        spread[r][0].wait_recv()
        one = links.send(rows_in.at[r, 3, 0], rows_in.at[r, 2, 0], xp)
        spread[r][1].wait_recv()
        two = links.send(rows_in.at[r, 1, 1], rows_in.at[r, 2, 1], xm)
        relay_x[r] = (one, two)

    act_x = {}

    def gate_up(r):
        for copy in relay_x[r]:
            copy.wait_recv()
        both = jnp.dot(
            rows_in[r, :, 0].reshape(4 * PAIR, 4 * STRIP), w_gu[0], preferred_element_type=F32
        ) + jnp.dot(
            rows_in[r, :, 1].reshape(4 * PAIR, 4 * STRIP), w_gu[1], preferred_element_type=F32
        )
        left, right = both[:, :384], both[:, 384:]
        made = (left / (1.0 + jnp.exp(-left)) * right).astype(BF).reshape(4, PAIR, 384)
        for slot in range(4):
            act[r, lax.rem(x + slot, 4), :, pl.ds(0, 384)] = made[slot]

    def spread_act(r):
        mine = act.at[r, :, :, pl.ds(0, 384)]
        act_x[r] = [
            links.send(mine, act.at[r, :, :, pl.ds((4 - dx) * 384, 384)], xs[dx])
            for dx in ((2, 1, 3) if r == LAST else (1, 3))
        ]

    def relay_act(r):
        for k, (device, slot) in enumerate(((xp, 3), (xm, 1))):
            act_x[r][k].wait_recv()
            half = pl.ds(2 * k, 2)
            act_x[r].append(
                links.send(
                    act.at[r, half, :, pl.ds(slot * 384, 384)], act.at[r, half, :, pl.ds(768, 384)], device
                )
            )

    home = {}

    def down(r):
        final = r == LAST
        for copy in act_x[r][-3 if final else -2:]:
            copy.wait_recv()
        whole = jnp.dot(
            act[r].reshape(4 * PAIR, 1536), w_dn[...], preferred_element_type=F32
        ).astype(BF).reshape(4, PAIR, 1280)
        for core in range(2):
            done[r, core] = whole[:, :, core * STRIP:(core + 1) * STRIP]
        slot = (4 - r) % 4
        if r == 0:
            home[0] = [links.send(done.at[0, 1 - c], back.at[0, c], sib)]
            back[0, c] = done[0, c]
        elif not final:
            home[slot] = links.send_both([done.at[r, 0], done.at[r, 1]], back.at[slot, c], chip(r), c)
        else:
            home[slot] = []
            for dx in (2, 1, 3, 0):
                t = lax.rem(x + dx, 4)
                home[slot].append(
                    links.send_both(
                        [done.at[r, 0, t], done.at[r, 1, t]], back.at[slot, c, t], chip(r), c
                    )
                )

    ending = (4 - LAST) % 4

    def wait_home():
        for copy in side["codes"]:
            copy.wait_recv()
        for slot in range(4):
            if slot != ending:
                for copy in home[slot]:
                    copy.wait_recv()

    over_x = {}

    def combine(dx):
        for copy in home[ending][(2, 1, 3, 0).index(dx)]:
            copy.wait_recv()
        t = lax.rem(x + dx, 4)
        mixed = lax.dot_general(
            pick(dx, (0, 1, 2, 3)),
            back[:, :, t].reshape(8 * PAIR, STRIP),
            (((0,), (0,)), ((), ())),
            preferred_element_type=F32,
        ).astype(BF)
        comb[dx] = mixed.reshape(2, 128, STRIP)
        if dx:
            over_x[4 - dx] = links.send_both(
                [comb.at[dx, 0], comb.at[dx, 1]], fin.at[4 - dx, c], chip(0, dx), c
            )
        else:
            over_x[0] = [links.send(comb.at[0, 1 - c], fin.at[0, c], sib)]
            fin[0, c] = comb[0, c]

    square = lax.broadcasted_iota(jnp.int32, (128, 128), 0) == lax.broadcasted_iota(
        jnp.int32, (128, 128), 1
    )
    weight = jnp.sum(jnp.where(square, gates[...], 0.0), axis=1, keepdims=True)
    stay = []

    def output(slot):
        if not stay:
            side["hid"].wait_recv()
        for copy in over_x[slot]:
            copy.wait_recv()
        b = lax.rem(x + slot, 4)
        cols = pl.ds(pl.multiple_of(b * STRIP, 128), STRIP)
        for half, rows in enumerate((hid.at[c], hid_sib)):
            core = c if half == 0 else 1 - c
            total = rows[:, cols] + weight * fin[slot, core].astype(F32)
            res[core, :, cols] = total.astype(BF)
            col = pl.ds(pl.multiple_of((2 * b + core) * STRIP, 128), STRIP)
            keep = pltpu.make_async_copy(
                res.at[core, :, cols], out.at[:, col], local_sems.at[2 * slot + half]
            )
            keep.start()
            stay.append(keep)

    step("siba", start_sibling)
    step("wdx", start_dn)
    step("wdz", share_dn)
    step("wdw", wait_dn)
    step("ownc", own_tokens)
    step("owns", sibling_tokens)
    step("code", place_tokens)
    step("codex", share_code)
    step("rs1own", first_half, "own")
    step("rs2own", second_half, "own")
    step("finown", finish_own)
    for j in range(n):
        step(f"sq{j}", start_q, j)
        step(f"sd{j}", start_d, j)
        step(f"onq{j}", on_q, j)
        step(f"onrq{j}", on_rq, j)
        step(f"ond{j}", on_d, j)
        step(f"onz{j}", on_z, j)
        step(f"onzo{j}", on_zo, j)
        step(f"sides{j}", sides, j)
        step(f"across{j}", across, j)
        step(f"rs1{j}", first_half, j)
        step(f"rs2{j}", second_half, j)
        step(f"fin{j}", finish_piece, j)
    step("share", start_share)
    step("other", start_other)
    step("norm", normalize)
    for r in range(4):
        step(f"disp{r}", dispatch, r)
        step(f"spread{r}", spread_rows, r)
        step(f"relay{r}", relay_rows, r)
        step(f"gu{r}", gate_up, r)
        step(f"act{r}", spread_act, r)
        step(f"ract{r}", relay_act, r)
        step(f"down{r}", down, r)
        step(f"comb{r}", combine, r)
        step(f"out{r}", output, r)
    step("homes", wait_home)
    for name in PLAN:
        steps.pop(name)()
    steps.pop(f"ract{LAST}")
    assert not steps
    for copy in stay:
        copy.wait()
    links.drain()


def scratch():
    wide = 3 * WIDE
    return [
        pltpu.VMEM((2, 512, 2048), BF),
        pltpu.VMEM((PIECES, 2048, WIDE), BF),
        pltpu.VMEM((PIECES, 3, 2048, WIDE), BF),
        pltpu.VMEM((2, 128, 4 * STRIP), BF),
        pltpu.VMEM((2, 128, 4 * STRIP), F32),
        pltpu.VMEM((128, 4 * STRIP), F32),
        pltpu.VMEM((4, 2, 128, STRIP), BF),
        pltpu.VMEM((PIECES, 4, 2, 128, wide), BF),
        pltpu.VMEM((2, 128, STRIP), BF),
        pltpu.VMEM((PIECES, 2, 128, wide), BF),
        pltpu.VMEM((2, 2, 128, STRIP), BF),
        pltpu.VMEM((PIECES, 2, 2, 128, wide), BF),
        pltpu.VMEM((2, 128, 128), F32),
        pltpu.VMEM((2, 128, 128), F32),
        pltpu.VMEM((4, 2, 8, 128), jnp.int32),
        pltpu.VMEM((2, 4 * STRIP, 768), BF),
        pltpu.VMEM((1536, 1280), BF),
        pltpu.VMEM((4, 2, PAIR, 4 * STRIP), BF),
        pltpu.VMEM((4, 4, 2, PAIR, 4 * STRIP), BF),
        pltpu.VMEM((4, 4, PAIR, 1536), BF),
        pltpu.VMEM((4, 2, 4, PAIR, STRIP), BF),
        pltpu.VMEM((4, 2, 4, PAIR, STRIP), BF),
        pltpu.VMEM((4, 2, 128, STRIP), BF),
        pltpu.VMEM((4, 2, 128, STRIP), BF),
        pltpu.SemaphoreType.DMA((SENDS,)),
        pltpu.SemaphoreType.DMA((SENDS,)),
        pltpu.SemaphoreType.DMA((40,)),
    ]


ANY = pl.BlockSpec(memory_space=pl.ANY)
VM = pl.BlockSpec(memory_space=pltpu.VMEM)


def shards(attn, w_out, resid, norm_gain, route_ids, gate_vals, w_gate, w_up, w_down):
    return pl.pallas_call(
        layer,
        out_shape=jax.ShapeDtypeStruct(resid.shape, BF),
        in_specs=[ANY, ANY, ANY, VM, VM, VM, ANY, ANY, ANY],
        out_specs=ANY,
        scratch_shapes=scratch(),
        compiler_params=pltpu.CompilerParams(
            collective_id=0, has_side_effects=True, vmem_limit_bytes=62 * 2**20
        ),
        name="layer",
    )(
        attn,
        w_out,
        resid,
        norm_gain.reshape(1, -1),
        route_ids.reshape(1, -1),
        gate_vals.reshape(1, -1),
        w_gate,
        w_up,
        w_down,
    )


def solution(mesh):
    placed = (
        P(("dp", "expert"), "tensor"),
        P("tensor", "expert"),
        P(("dp", "expert", "tensor"), None),
        P(),
        P(("dp", "expert", "tensor"), None),
        P(("dp", "expert", "tensor"), None),
        P("expert", None, "tensor"),
        P("expert", None, "tensor"),
        P("expert", "tensor", None),
    )
    return jax.shard_map(
        shards,
        mesh=mesh,
        in_specs=placed,
        out_specs=P(("dp", "expert", "tensor"), None),
        check_vma=False,
    )
```

time: 218 us -> 190 us (0.87)
  Pallas kernels: 211 us -> 187 us
  other arithmetic: 2.4 us -> 0 us
    pallas_call x1, Pallas kernels: 211 us -> 187 us  [shards(): pl.pallas_call(layer, out_shape=jax.ShapeDtypeStruct(resid.shape, BF), in...]
where the time goes in v3:
time: 190 us
  Pallas kernels  187 us (98%)
  local copies, waits for them, and re-layouts  2.46 us (1%)
    pallas_call x1, Pallas kernels, shards(): pl.pallas_call(layer, out_shape=jax.ShapeDtypeStruct(resid.shape, BF), in...  187 us

profile of v3, /device:TPU:1, one launch (start us, length us, event | category | flops | bytes accessed | tf_op | source)
XLA Modules:
  0.0 189.7 jit_solution(16277225692970642838)
XLA Ops:
  0.0 187.3 %layer.1 = bf16[128,5120]{1,0:T(8,128)(2,1)} custom-call(bf16[512,2048]{1,0:T(8,128)(2,1)} %attn.1, bf16[2048,640]{1,0:T(8,128)(2,1)} %w_out.1, bf16[128,5120]{1,0:T(8,128)(2,1)} %resid.1, f32[1,5120]{1,0:T(1,128)} %bitcast.3, s32[1,128]{1,0:T(1,128)} %bitcast.4, f32[1,128]{1,0:T(1,128)} %bitcast.5, bf16[1,5120,384]{2,1,0:T(8,128)(2,1)} %w_gate.1, ...), custom_call_target="tpu_custom_call" | custom-call | tf_op jit(solution)/shard_map/layer/pallas_call | solution.py:677
  187.3 2.5 %copy.11 = bf16[128,5120]{1,0:T(8,128)(2,1)} copy(bf16[128,5120]{1,0:T(8,128)(2,1)} %layer.1) | data formatting | bytes 2621440

commit v4 on v3

v4 whole, which is shorter than its diff:
```python
import functools

import jax
import jax.numpy as jnp
from jax import lax
from jax.experimental import pallas as pl
from jax.experimental.pallas import tpu as pltpu
from jax.sharding import PartitionSpec as P

MESH = pl.DeviceIdType.MESH
BF = jnp.bfloat16
F32 = jnp.float32

QN = 336
DN = 2048 - 4 * QN
QH = 176
PIECES = 5
WIDE = 128
STRIP = 640
FRONT = 2 * STRIP


class Place:
    def __init__(self):
        self.z = lax.axis_index("dp")
        self.e = lax.axis_index("expert")
        self.x = lax.axis_index("tensor")
        self.y = self.e // 2
        self.c = self.e % 2

    def at(self, dx=0, dy=0, dz=0, flip=False):
        core = 1 - self.c if flip else self.c
        return (
            lax.rem(self.z + dz, 4),
            lax.rem(self.y + dy, 4) * 2 + core,
            lax.rem(self.x + dx, 4),
        )


class Links:
    def __init__(self, send_sems, recv_sems):
        self.send_sems, self.recv_sems = send_sems, recv_sems
        self.free, self.made, self.landings, self.open = [], 0, 0, []

    def landing(self):
        self.landings += 1
        return self.landings - 1

    def send(self, src, dst, device, landing=None):
        if not self.free:
            self.free.append(self.made)
            self.made += 1
        i = self.free.pop(0)
        copy = pltpu.make_async_remote_copy(
            src_ref=src,
            dst_ref=dst,
            send_sem=self.send_sems.at[i],
            recv_sem=self.recv_sems.at[self.landing() if landing is None else landing],
            device_id=device,
            device_id_type=MESH,
        )
        copy.start()
        self.open.append((copy, i))
        return copy

    def send_both(self, sources, dst, devices, landing):
        for source, device in zip(sources, devices):
            self.send(source, dst, device, landing)

    def landed(self, landing, dst, device):
        pltpu.make_async_remote_copy(
            src_ref=dst,
            dst_ref=dst,
            send_sem=self.send_sems.at[0],
            recv_sem=self.recv_sems.at[landing],
            device_id=device,
            device_id_type=MESH,
        ).wait_recv()

    def settle(self, count):
        done, self.open = self.open[:count], self.open[count:]
        for copy, i in done:
            copy.wait_send()
            self.free.append(i)

    def settle_through(self, last):
        for k, (copy, _) in enumerate(self.open):
            if copy is last:
                self.settle(k + 1)
                return

    def settle_all_but(self, count):
        self.settle(max(0, len(self.open) - count))


def greet(devices):
    for device in devices:
        pl.semaphore_signal(
            pltpu.get_barrier_semaphore(), inc=1, device_id=device, device_id_type=MESH
        )


SENDS = 92
LANDINGS = 167
KEEP = 48
CAP = 24
PAIR = 2 * CAP
LAST = 3
OWN = PIECES
(
    TO_SIBLING, DOWN_X, DOWN_Z, DOWN_WAIT, OWN_TOKENS, SIBLING_TOKENS, PLACE, PLACE_X, PLACE_WAIT, SUM_SEND,
    SUM_AHEAD, SUM_BEHIND, SUM_END, SEND_Q, SEND_D, Q_BEHIND, Q_AHEAD, Q_ACROSS, D_HERE, Z_BEHIND, Z_AHEAD,
    Z_ACROSS, MUL_SIDES, MUL_ACROSS, SQUARES, HIDDEN, NORM, ROWS_Y, ROWS_X, ROWS_AHEAD, ROWS_BEHIND, SHOW,
    SHOW_AHEAD, SHOW_BEHIND, SHOW_WAIT, SHOWN_Y, SHOWN_WAIT, GATE_UP, ACT_X, ACT_RELAY, DOWN, HOME, COMBINE,
    OUT,
) = range(44)
PLAN = (
    (SEND_Q, 0), (TO_SIBLING,), (OWN_TOKENS,), (SEND_Q, 2), (Q_BEHIND, 0), (Q_AHEAD, 0), (DOWN_X,),
    (SEND_Q, 1), (SEND_D, 2), (Q_BEHIND, 2), (Q_AHEAD, 2), (PLACE,), (Z_AHEAD, 0), (SEND_D, 0),
    (Q_BEHIND, 1), (SEND_D, 1), (SIBLING_TOKENS,), (Q_ACROSS, 2), (Q_AHEAD, 1), (SUM_SEND, OWN),
    (Z_BEHIND, 2), (D_HERE, 2), (Z_AHEAD, 2), (Q_ACROSS, 0), (Z_ACROSS, 2), (Z_BEHIND, 1), (SEND_Q, 4),
    (SUM_AHEAD, OWN), (PLACE_X,), (SUM_BEHIND, OWN), (Z_BEHIND, 0), (D_HERE, 0), (Q_ACROSS, 1),
    (MUL_SIDES, 2), (Z_ACROSS, 0), (D_HERE, 1), (MUL_ACROSS, 2), (SUM_SEND, 2), (Q_BEHIND, 4), (Q_AHEAD, 4),
    (SEND_Q, 3), (MUL_SIDES, 0), (Z_AHEAD, 1), (SEND_D, 4), (MUL_ACROSS, 0), (SUM_END, OWN), (SUM_SEND, 0),
    (Z_ACROSS, 1), (Q_ACROSS, 4), (Z_BEHIND, 4), (Z_AHEAD, 4), (SUM_AHEAD, 2), (Q_BEHIND, 3), (Q_AHEAD, 3),
    (SEND_D, 3), (SUM_BEHIND, 2), (PLACE_WAIT,), (MUL_SIDES, 1), (MUL_ACROSS, 1), (SUM_SEND, 1), (D_HERE, 4),
    (Z_ACROSS, 4), (Q_ACROSS, 3), (MUL_SIDES, 4), (Z_BEHIND, 3), (SUM_BEHIND, 0), (SUM_AHEAD, 0),
    (D_HERE, 3), (Z_AHEAD, 3), (SUM_AHEAD, 1), (SUM_BEHIND, 1), (MUL_ACROSS, 4), (Z_ACROSS, 3),
    (SUM_SEND, 4), (MUL_SIDES, 3), (MUL_ACROSS, 3), (SUM_SEND, 3), (SUM_BEHIND, 4), (DOWN_Z,), (SUM_END, 0),
    (SUM_END, 2), (SUM_AHEAD, 4), (SUM_AHEAD, 3), (SUM_BEHIND, 3), (SUM_END, 1), (SUM_END, 4), (SUM_END, 3),
    (SQUARES,), (NORM,), (ROWS_Y, 2), (SHOW,), (ROWS_Y, 0), (SHOWN_Y, 0, 0), (SHOWN_Y, 1, 0), (ROWS_X, 2),
    (SHOWN_Y, 2, 0), (ROWS_Y, 3), (ROWS_Y, 1), (SHOW_BEHIND,), (SHOW_AHEAD,), (SHOWN_Y, 2, 1),
    (ROWS_BEHIND, 2), (ROWS_X, 1), (SHOWN_Y, 2, 3), (ROWS_AHEAD, 2), (SHOW_WAIT,), (ROWS_X, 0),
    (SHOWN_Y, 2, 2), (ROWS_AHEAD, 1), (SHOWN_Y, 1, 2), (SHOWN_Y, 1, 1), (SHOWN_Y, 0, 1), (SHOWN_Y, 1, 3),
    (SHOWN_Y, 0, 3), (SHOWN_Y, 3, 1), (ROWS_BEHIND, 1), (SHOWN_Y, 3, 0), (SHOWN_WAIT, 2), (GATE_UP, 2),
    (ACT_X, 2), (SHOWN_Y, 0, 2), (SHOWN_Y, 3, 3), (ROWS_X, 3), (ACT_RELAY, 2), (ROWS_BEHIND, 0),
    (ROWS_AHEAD, 0), (SHOWN_Y, 3, 2), (ROWS_BEHIND, 3), (ROWS_AHEAD, 3), (SHOWN_WAIT, 1), (SHOWN_WAIT, 0),
    (DOWN_WAIT,), (GATE_UP, 1), (ACT_X, 1), (DOWN, 2), (GATE_UP, 0), (ACT_X, 0), (SHOWN_WAIT, 3),
    (GATE_UP, 3), (ACT_RELAY, 1), (ACT_X, 3), (DOWN, 1), (HIDDEN,), (ACT_RELAY, 0), (DOWN, 3), (DOWN, 0),
    (HOME,), (COMBINE, 2), (COMBINE, 1), (COMBINE, 0), (COMBINE, 3), (OUT, 2), (OUT, 0), (OUT, 3), (OUT, 1),
)


def layer(
    attn, w_out, resid, gain, ids, gates, w_gate, w_up, w_down, out,
    a_buf, w_own, w, res, hid, hid_sib, p_own, parts, l_own, relays, f_own, finals,
    ssq, ssq_sib, code, w_gu, w_dn, rows_in, near, sown, act, done, back, fin,
    send_sems, recv_sems, local_sems,
):
    me = Place()
    z, x, y, c = me.z, me.x, me.y, me.c
    sib = me.at(flip=True)
    xp, xm, xo = me.at(dx=1), me.at(dx=3), me.at(dx=2)
    yp, ym, zp, zm = me.at(dy=1), me.at(dy=3), me.at(dz=1), me.at(dz=3)
    links = Links(send_sems, recv_sems)

    def chip(dy, dx=0):
        return [(z, lax.rem(y + dy, 4) * 2 + core, lax.rem(x + dx, 4)) for core in range(2)]

    zo_, xs = me.at(dz=2), (None, xp, xo, xm)
    friends = [sib, *chip(1), *chip(2), *chip(3), zp, zm, zo_, *chip(0, 1), *chip(0, 2), *chip(0, 3)]
    greet(friends)

    load_w = [
        pltpu.make_async_copy(w_out.at[:, pl.ds(j * WIDE, WIDE)], w_own.at[j], local_sems.at[j])
        for j in range(PIECES)
    ]
    for load in load_w:
        load.start()
    load_a = pltpu.make_async_copy(attn, a_buf.at[c], local_sems.at[5])
    load_a.start()
    for b in range(4):
        col = pl.multiple_of((2 * b + c) * STRIP, 128)
        load = pltpu.make_async_copy(
            resid.at[:, pl.ds(col, STRIP)], res.at[c, :, pl.ds(b * STRIP, STRIP)], local_sems.at[6]
        )
        load.start()

    loads = []
    for half in range(2):
        for b in range(4):
            source = pl.ds((2 * b + half) * STRIP, STRIP)
            target = pl.ds(b * STRIP, STRIP)
            for k, weight in enumerate((w_gate, w_up)):
                loads.append((weight.at[0, source], w_gu.at[half, target, pl.ds(k * 384, 384)]))
    quarter = pl.ds(pl.multiple_of(x * 1280, 128), 1280)
    loads.append((w_down.at[0, :, quarter], w_dn.at[pl.ds(0, 384)]))
    loads = [
        pltpu.make_async_copy(source, target, local_sems.at[7 if k < 16 else 8])
        for k, (source, target) in enumerate(loads)
    ]

    pl.semaphore_wait(pltpu.get_barrier_semaphore(), len(friends))
    for load in loads:
        load.start()

    def rows_q(half=None):
        start = z * QN
        if half is None:
            return pl.ds(pl.multiple_of(start, 16), QN)
        return pl.ds(pl.multiple_of(start + half * QH, 16), QN - QH if half else QH)

    rows_d = pl.ds(4 * QN, DN)

    def rows_dh(half):
        return pl.ds(4 * QN + half * (DN // 2), DN // 2)

    def own(j, rows):
        return w_own.at[j, rows]

    def send_q(j):
        return (
            links.send(own(j, rows_q()), w.at[j, 1, rows_q()], yp),
            links.send(own(j, rows_q()), w.at[j, 0, rows_q()], ym),
        )

    def send_d(j):
        return (
            links.send(own(j, rows_d), w.at[j, 1, rows_d], yp),
            links.send(own(j, rows_d), w.at[j, 0, rows_d], ym),
        )

    n = PIECES
    q, d, zs, zo, side, first, front, lands = ({} for _ in range(8))
    rows_far = pl.ds(pl.multiple_of(lax.rem(z + 2, 4) * QN, 16), QN)

    def land(*key):
        if key not in lands:
            lands[key] = links.landing()
        return lands[key]

    steps = {}

    def step(kind, run, *args, given=None):
        steps[(kind, *(args if given is None else given))] = functools.partial(run, *args)

    loaded = set()

    def need(j):
        if j not in loaded:
            load_w[j].wait()
            loaded.add(j)

    def start_q(j):
        need(j)
        q[j] = send_q(j)

    def start_d(j):
        need(j)
        d[j] = send_d(j)

    def start_sibling():
        side["attn"] = links.send(attn, a_buf.at[c], sib)
        side["resid"] = links.landing()
        for b in range(4):
            col = pl.multiple_of((2 * b + 1 - c) * STRIP, 128)
            links.send(
                resid.at[:, pl.ds(col, STRIP)], res.at[c, :, pl.ds(b * STRIP, STRIP)], sib, side["resid"]
            )

    dn_rows = pl.multiple_of(z * 96, 16)
    dn_x, dn_z = {}, []

    def start_dn():
        for dx in (1, 3, 2):
            column = pl.multiple_of(lax.rem(x + dx, 4) * 1280, 128)
            dn_x[4 - dx] = links.send(
                w_down.at[0, pl.ds(dn_rows, 96), pl.ds(column, 1280)],
                w_dn.at[pl.ds((4 - dx) * 384 + dn_rows, 96)],
                xs[dx],
            )

    def share_dn():
        for slot in (3, 1, 2):
            dn_x[slot].wait_recv()
            piece = w_dn.at[pl.ds(slot * 384 + dn_rows, 96)]
            dn_z.extend(links.send(piece, piece, device) for device in (zp, zm, zo_))

    def wait_dn():
        for copy in dn_z:
            copy.wait_recv()

    def multiply(blocks, part, core, col):
        def step(m, carry):
            rows = pl.ds(pl.multiple_of(m * 256, 256), 256)
            right = blocks[0][...]
            if len(blocks) > 1:
                right = jnp.concatenate([block[...] for block in blocks], axis=1)
            result = jnp.dot(a_buf[core, rows, :], right, preferred_element_type=F32).astype(BF)
            cols = pl.ds(col, right.shape[1])
            part[2 * m, core, :, cols] = result[:128]
            part[2 * m + 1, core, :, cols] = result[128:]
            return carry

        lax.fori_loop(0, 2, step, 0)

    ahead, behind, over = lax.rem(x + 1, 4), lax.rem(x + 3, 4), lax.rem(x + 2, 4)

    def group(j):
        return (p_own, l_own, f_own) if j == OWN else (parts.at[j], relays.at[j], finals.at[j])

    def reduce_first(j):
        part, relay, final = group(j)
        first[j] = (
            links.send(part.at[over, 0], relay.at[0], xp),
            links.send(part.at[over, 1], relay.at[1], xm),
        )
        links.send(part.at[ahead, 1], final.at[0, 1], xp, land(j, "sum"))
        links.send(part.at[behind, 0], final.at[1, 0], xm, land(j, "sum"))

    def reduce_ahead(j):
        part, relay, final = group(j)
        first[j][0].wait_recv()
        part[ahead, 0] = (part[ahead, 0].astype(F32) + relay[0].astype(F32)).astype(BF)
        front[j, 0] = links.send(part.at[ahead, 0], final.at[0, 0], xp, land(j, "sum"))

    def reduce_behind(j):
        part, relay, final = group(j)
        first[j][1].wait_recv()
        part[behind, 1] = (part[behind, 1].astype(F32) + relay[1].astype(F32)).astype(BF)
        front[j, 1] = links.send(part.at[behind, 1], final.at[1, 1], xm, land(j, "sum"))

    def on_q_behind(j):
        q[j][0].wait_recv()
        links.send(w.at[j, 1, rows_q(0)], w.at[j, 2, rows_q(0)], yp, land(j, "rq"))
        zs[j, 1] = (
            links.send(w.at[j, 1, rows_q()], w.at[j, 1, rows_q()], zp),
            links.send(w.at[j, 1, rows_q()], w.at[j, 1, rows_q()], zm),
        )

    def on_q_ahead(j):
        q[j][1].wait_recv()
        links.send(w.at[j, 0, rows_q(1)], w.at[j, 2, rows_q(1)], ym, land(j, "rq"))
        zs[j, 0] = (
            links.send(w.at[j, 0, rows_q()], w.at[j, 0, rows_q()], zp),
            links.send(w.at[j, 0, rows_q()], w.at[j, 0, rows_q()], zm),
        )

    def on_rq(j):
        links.landed(land(j, "rq"), w.at[j, 2, rows_q()], yp)
        zo[j] = (
            links.send(w.at[j, 2, rows_q()], w.at[j, 2, rows_q()], zp),
            links.send(w.at[j, 2, rows_q()], w.at[j, 2, rows_q()], zm),
        )

    def on_d(j):
        d[j][0].wait_recv()
        links.send(w.at[j, 1, rows_dh(0)], w.at[j, 2, rows_dh(0)], yp, land(j, "rd"))
        d[j][1].wait_recv()
        links.send(w.at[j, 0, rows_dh(1)], w.at[j, 2, rows_dh(1)], ym, land(j, "rd"))

    def z_relay(j, pair, slot):
        low = pl.ds(pl.multiple_of(lax.rem(z + 3, 4) * QN, 16), QH)
        high = pl.ds(pl.multiple_of(lax.rem(z + 1, 4) * QN + QH, 16), QN - QH)
        pair[0].wait_recv()
        links.send(w.at[j, slot, low], w.at[j, slot, low], zp, land(j, slot))
        pair[1].wait_recv()
        links.send(w.at[j, slot, high], w.at[j, slot, high], zm, land(j, slot))

    def on_z(j, slot):
        z_relay(j, zs[j, slot], slot)

    def on_zo(j):
        z_relay(j, zo[j], 2)

    def sides(j):
        links.landed(land(j, 0), w.at[j, 0, rows_far], zp)
        links.landed(land(j, 1), w.at[j, 1, rows_far], zp)
        for core in range(2):
            multiply([w.at[j, 0], w.at[j, 1]], parts.at[j], core, 0)

    def across(j):
        links.landed(land(j, "rd"), w.at[j, 2, rows_d], yp)
        links.landed(land(j, 2), w.at[j, 2, rows_far], zp)
        links.settle_all_but(KEEP)
        for core in range(2):
            multiply([w.at[j, 2]], parts.at[j], core, 2 * WIDE)

    own_pieces = [w_own.at[j] for j in range(PIECES)]

    def own_tokens():
        load_a.wait()
        for j in range(n):
            need(j)
        multiply(own_pieces, p_own, c, 0)

    def sibling_tokens():
        side["attn"].wait_recv()
        multiply(own_pieces, p_own, 1 - c, 0)

    def place_tokens():
        experts = lax.broadcasted_iota(jnp.int32, (8, 128), 0)
        named = ids[...] == experts
        counts = named.astype(F32)
        before = lax.broadcasted_iota(jnp.int32, (128, 128), 0) < lax.broadcasted_iota(
            jnp.int32, (128, 128), 1
        )
        earlier = jnp.dot(counts.astype(BF), before.astype(F32).astype(BF), preferred_element_type=F32)
        slots = jnp.sum(jnp.where(named, earlier, 0.0), axis=0, keepdims=True).astype(jnp.int32)
        code[0, c] = jnp.broadcast_to(ids[...] * PAIR + c * CAP + slots, (8, 128))
        side["code"] = links.send(code.at[0, c], code.at[0, c], sib)

    def share_code():
        side["code"].wait_recv()
        side["codes"] = [links.send(code.at[0], code.at[4 - dx], xs[dx]) for dx in (1, 3, 2)]

    def finish(j, strips, width):
        part, _, final = group(j)
        links.landed(land(j, "sum"), final, xp)
        for k, (col, strip) in enumerate(strips):
            cols = pl.ds(col, width)
            for core in range(2):
                at = pl.ds(k * width, width)
                total = (
                    res[core, :, cols].astype(F32)
                    + part[x, core, :, at].astype(F32)
                    + final[0, core, :, at].astype(F32)
                    + final[1, core, :, at].astype(F32)
                )
                hid[core, :, cols] = total
                add = jnp.sum(total * total, axis=1, keepdims=True)
                ssq[core] = ssq[core] + jnp.broadcast_to(add, (128, 128))

    ssq[...] = jnp.zeros_like(ssq)

    def finish_piece(j):
        strips = [
            (pl.multiple_of(lax.rem(y + dy, 4) * STRIP + j * WIDE, 128), k)
            for k, dy in enumerate((1, 3, 2))
        ]
        finish(j, strips, WIDE)

    def finish_own(_):
        pltpu.make_async_copy(res.at[c], res.at[c], local_sems.at[6]).wait()
        links.landed(side["resid"], res.at[1 - c], sib)
        finish(OWN, [(pl.multiple_of(y * STRIP, 128), 0)], STRIP)

    def start_share():
        side["ssq"] = links.send(ssq, ssq_sib, sib)

    def start_other():
        side["hid"] = links.send(hid.at[1 - c], hid_sib, sib)


    def pick(slot, chips):
        blocks = []
        for dy in chips:
            base = lax.rem(y + dy, 4) * (2 * PAIR)
            place = base + lax.broadcasted_iota(jnp.int32, (2 * PAIR, 128), 0)
            blocks.append(
                jnp.concatenate(
                    [
                        (place == code[slot, core, 0:1, :]).astype(F32).astype(BF)
                        for core in range(2)
                    ],
                    axis=1,
                )
            )
        return blocks[0] if len(blocks) == 1 else jnp.concatenate(blocks, axis=0)

    def normalize():
        side["ssq"].wait_recv()
        for core in range(2):
            scale = lax.rsqrt((ssq[core] + ssq_sib[core])[:, 0:1] / 5120.0 + 1e-06)
            for b in range(4):
                cols = pl.ds(b * STRIP, STRIP)
                col = pl.multiple_of((2 * b + c) * STRIP, 128)
                res[core, :, cols] = (hid[core, :, cols] * scale * gain[0:1, pl.ds(col, STRIP)]).astype(BF)
        pltpu.make_async_copy(w_gu, w_gu, local_sems.at[7]).wait()
        loads[16].wait()
        links.settle_all_but(KEEP)

    arrive, come, shown = {}, {}, []
    early, later = pl.ds(0, FRONT), pl.ds(FRONT, FRONT)

    def sent(dy, core):
        return a_buf.at[0, pl.ds(pl.multiple_of((2 * dy + core) * PAIR, 16), PAIR), early]

    def dispatch(r):
        dy = (4 - r) % 4
        choice = pick(0, (dy,))
        normed = res[:, :, later].reshape(256, FRONT)
        rows = jnp.dot(choice, normed, preferred_element_type=F32).astype(BF)
        a_buf[0, pl.ds(2 * dy * PAIR, 2 * PAIR), early] = rows
        slot = (4 - dy) % 4
        if dy == 0:
            arrive[0] = links.send(sent(0, 1 - c), rows_in.at[0, 0, c, :, later], sib)
            rows_in[0, 0, c, :, later] = sent(0, c)[...]
        else:
            target = rows_in.at[slot, 0, c, :, later]
            links.send_both([sent(dy, 0), sent(dy, 1)], target, chip(dy), land("rows", slot))

    spread, relay_x = {}, {}

    def show_rows():
        shown.append(links.send(res.at[:, :, early], near.at[2], xp))
        shown.append(links.send(res.at[:, :, early], near.at[0], xm))
        front["shown"] = shown[-1]

    def show_on_ahead():
        shown[0].wait_recv()
        come[0] = links.send(near.at[2, 0], near.at[1, 0], xp)

    def show_on_behind():
        shown[1].wait_recv()
        come[1] = links.send(near.at[0, 1], near.at[1, 1], xm)

    def wait_shown():
        come[0].wait_recv()
        come[1].wait_recv()

    def dispatch_shown(r, t):
        dy = (4 - r) % 4
        source = res[:, :, early] if t == 0 else near[t - 1]
        rows = jnp.dot(pick(t, (dy,)), source.reshape(256, FRONT), preferred_element_type=F32)
        sown[r, t] = rows.astype(BF).reshape(2, PAIR, FRONT)
        target = rows_in.at[r, t, c, :, early]
        if r == 0:
            links.send(sown.at[r, t, 1 - c], target, sib, land("shown", r))
            rows_in[r, t, c, :, early] = sown[r, t, c]
        else:
            links.send_both([sown.at[r, t, 0], sown.at[r, t, 1]], target, chip(dy), land("shown", r))

    def wait_dispatched(r):
        links.settle_all_but(KEEP)
        whole = rows_in.at[0, :, 1 - c, :, early] if r == 0 else rows_in.at[r, :, :, :, early]
        links.landed(land("shown", r), whole, sib)

    spread, relay_x = {}, {}

    def spread_rows(r):
        if r == 0:
            arrive[0].wait_recv()
        else:
            links.landed(land("rows", r), rows_in.at[r, 0, :, :, later], sib)
        mine = rows_in.at[r, 0, :, :, later]
        spread[r] = (
            links.send(mine, rows_in.at[r, 3, :, :, later], xp),
            links.send(mine, rows_in.at[r, 1, :, :, later], xm),
        )

    def relay_ahead(r):
        spread[r][0].wait_recv()
        relay_x[r, 0] = links.send(rows_in.at[r, 3, 0, :, later], rows_in.at[r, 2, 0, :, later], xp)

    def relay_behind(r):
        spread[r][1].wait_recv()
        relay_x[r, 1] = links.send(rows_in.at[r, 1, 1, :, later], rows_in.at[r, 2, 1, :, later], xm)

    act_x = {}

    def gate_up(r):
        relay_x[r, 0].wait_recv()
        relay_x[r, 1].wait_recv()
        links.settle_all_but(KEEP)
        both = jnp.dot(
            rows_in[r, :, 0].reshape(4 * PAIR, 4 * STRIP), w_gu[0], preferred_element_type=F32
        ) + jnp.dot(
            rows_in[r, :, 1].reshape(4 * PAIR, 4 * STRIP), w_gu[1], preferred_element_type=F32
        )
        left, right = both[:, :384], both[:, 384:]
        made = (left / (1.0 + jnp.exp(-left)) * right).astype(BF).reshape(4, PAIR, 384)
        for slot in range(4):
            act[r, lax.rem(x + slot, 4), :, pl.ds(0, 384)] = made[slot]

    def spread_act(r):
        mine = act.at[r, :, :, pl.ds(0, 384)]
        act_x[r] = [
            links.send(mine, act.at[r, :, :, pl.ds((4 - dx) * 384, 384)], xs[dx])
            for dx in ((2, 1, 3) if r == LAST else (1, 3))
        ]

    def relay_act(r):
        for k, (device, slot) in enumerate(((xp, 3), (xm, 1))):
            act_x[r][k].wait_recv()
            half = pl.ds(2 * k, 2)
            act_x[r].append(
                links.send(
                    act.at[r, half, :, pl.ds(slot * 384, 384)], act.at[r, half, :, pl.ds(768, 384)], device
                )
            )

    home = {}

    def down(r):
        final = r == LAST
        for copy in act_x[r][-3 if final else -2:]:
            copy.wait_recv()
        whole = jnp.dot(
            act[r].reshape(4 * PAIR, 1536), w_dn[...], preferred_element_type=F32
        ).astype(BF).reshape(4, PAIR, 1280)
        for core in range(2):
            done[r, core] = whole[:, :, core * STRIP:(core + 1) * STRIP]
        slot = (4 - r) % 4
        if r == 0:
            home[0] = links.send(done.at[0, 1 - c], back.at[0, c], sib)
            back[0, c] = done[0, c]
        elif not final:
            links.send_both(
                [done.at[r, 0], done.at[r, 1]], back.at[slot, c], chip(r), land("home", slot)
            )
        else:
            for dx in (2, 1, 3, 0):
                t = lax.rem(x + dx, 4)
                links.send_both(
                    [done.at[r, 0, t], done.at[r, 1, t]], back.at[slot, c, t], chip(r), land("end", dx)
                )

    ending = (4 - LAST) % 4

    def wait_codes():
        for copy in side["codes"]:
            copy.wait_recv()

    def wait_home():
        for slot in range(4):
            if slot == 0:
                home[0].wait_recv()
            elif slot != ending:
                links.landed(land("home", slot), back.at[slot], sib)


    comb = p_own

    def combine(dx):
        t = lax.rem(x + dx, 4)
        links.settle_through(front[OWN, 0])
        links.settle_through(front[OWN, 1])
        links.landed(land("end", dx), back.at[ending, :, t], sib)
        mixed = lax.dot_general(
            pick(dx, (0, 1, 2, 3)),
            back[:, :, t].reshape(8 * PAIR, STRIP),
            (((0,), (0,)), ((), ())),
            preferred_element_type=F32,
        ).astype(BF)
        comb[dx] = mixed.reshape(2, 128, STRIP)
        if dx:
            links.send_both(
                [comb.at[dx, 0], comb.at[dx, 1]], fin.at[4 - dx, c], chip(0, dx), land("out", 4 - dx)
            )
        else:
            links.send(comb.at[0, 1 - c], fin.at[0, c], sib, land("out", 0))
            fin[0, c] = comb[0, c]

    square = lax.broadcasted_iota(jnp.int32, (128, 128), 0) == lax.broadcasted_iota(
        jnp.int32, (128, 128), 1
    )
    weight = jnp.sum(jnp.where(square, gates[...], 0.0), axis=1, keepdims=True)
    stay = []

    def output(slot):
        if not stay:
            side["hid"].wait_recv()
            links.settle_through(front["shown"])
        stay.append(slot)
        links.landed(land("out", slot), fin.at[0, 1 - c] if slot == 0 else fin.at[slot], sib)
        b = lax.rem(x + slot, 4)
        cols = pl.ds(pl.multiple_of(b * STRIP, 128), STRIP)
        for half, rows in enumerate((hid.at[c], hid_sib)):
            core = c if half == 0 else 1 - c
            total = rows[:, cols] + weight * fin[slot, core].astype(F32)
            res[core, :, cols] = total.astype(BF)
            col = pl.ds(pl.multiple_of((2 * b + core) * STRIP, 128), STRIP)
            keep = pltpu.make_async_copy(
                res.at[core, :, cols], out.at[:, col], local_sems.at[9]
            )
            keep.start()

    step(TO_SIBLING, start_sibling)
    step(DOWN_X, start_dn)
    step(DOWN_Z, share_dn)
    step(DOWN_WAIT, wait_dn)
    step(OWN_TOKENS, own_tokens)
    step(SIBLING_TOKENS, sibling_tokens)
    step(PLACE, place_tokens)
    step(PLACE_X, share_code)
    step(SUM_SEND, reduce_first, OWN)
    step(SUM_AHEAD, reduce_ahead, OWN)
    step(SUM_BEHIND, reduce_behind, OWN)
    step(SUM_END, finish_own, OWN)
    for j in range(n):
        step(SEND_Q, start_q, j)
        step(SEND_D, start_d, j)
        step(Q_BEHIND, on_q_behind, j)
        step(Q_AHEAD, on_q_ahead, j)
        step(Q_ACROSS, on_rq, j)
        step(D_HERE, on_d, j)
        step(Z_BEHIND, on_z, j, 1, given=(j,))
        step(Z_AHEAD, on_z, j, 0, given=(j,))
        step(Z_ACROSS, on_zo, j)
        step(MUL_SIDES, sides, j)
        step(MUL_ACROSS, across, j)
        step(SUM_SEND, reduce_first, j)
        step(SUM_AHEAD, reduce_ahead, j)
        step(SUM_BEHIND, reduce_behind, j)
        step(SUM_END, finish_piece, j)
    step(SQUARES, start_share)
    step(HIDDEN, start_other)
    step(NORM, normalize)
    for r in range(4):
        step(ROWS_Y, dispatch, r)
        step(ROWS_X, spread_rows, r)
        step(ROWS_AHEAD, relay_ahead, r)
        step(ROWS_BEHIND, relay_behind, r)
        step(SHOWN_WAIT, wait_dispatched, r)
        for t in range(4):
            step(SHOWN_Y, dispatch_shown, r, t)
        step(GATE_UP, gate_up, r)
        step(ACT_X, spread_act, r)
        step(ACT_RELAY, relay_act, r)
        step(DOWN, down, r)
        step(COMBINE, combine, r)
        step(OUT, output, r)
    step(HOME, wait_home)
    step(PLACE_WAIT, wait_codes)
    step(SHOW, show_rows)
    step(SHOW_AHEAD, show_on_ahead)
    step(SHOW_BEHIND, show_on_behind)
    step(SHOW_WAIT, wait_shown)
    for key in PLAN:
        steps.pop(key)()
    steps.pop((ACT_RELAY, LAST))
    assert not steps
    pltpu.make_async_copy(out, out, local_sems.at[9]).wait()
    links.settle_all_but(0)


def scratch():
    wide = 3 * WIDE
    return [
        pltpu.VMEM((2, 512, 2048), BF),
        pltpu.VMEM((PIECES, 2048, WIDE), BF),
        pltpu.VMEM((PIECES, 3, 2048, WIDE), BF),
        pltpu.VMEM((2, 128, 4 * STRIP), BF),
        pltpu.VMEM((2, 128, 4 * STRIP), F32),
        pltpu.VMEM((128, 4 * STRIP), F32),
        pltpu.VMEM((4, 2, 128, STRIP), BF),
        pltpu.VMEM((PIECES, 4, 2, 128, wide), BF),
        pltpu.VMEM((2, 128, STRIP), BF),
        pltpu.VMEM((PIECES, 2, 128, wide), BF),
        pltpu.VMEM((2, 2, 128, STRIP), BF),
        pltpu.VMEM((PIECES, 2, 2, 128, wide), BF),
        pltpu.VMEM((2, 128, 128), F32),
        pltpu.VMEM((2, 128, 128), F32),
        pltpu.VMEM((4, 2, 8, 128), jnp.int32),
        pltpu.VMEM((2, 4 * STRIP, 768), BF),
        pltpu.VMEM((1536, 1280), BF),
        pltpu.VMEM((4, 4, 2, PAIR, 4 * STRIP), BF),
        pltpu.VMEM((3, 2, 128, FRONT), BF),
        pltpu.VMEM((4, 4, 2, PAIR, FRONT), BF),
        pltpu.VMEM((4, 4, PAIR, 1536), BF),
        pltpu.VMEM((4, 2, 4, PAIR, STRIP), BF),
        pltpu.VMEM((4, 2, 4, PAIR, STRIP), BF),
        pltpu.VMEM((4, 2, 128, STRIP), BF),
        pltpu.SemaphoreType.DMA((SENDS,)),
        pltpu.SemaphoreType.DMA((LANDINGS,)),
        pltpu.SemaphoreType.DMA((10,)),
    ]


ANY = pl.BlockSpec(memory_space=pl.ANY)
VM = pl.BlockSpec(memory_space=pltpu.VMEM)


def shards(attn, w_out, resid, norm_gain, route_ids, gate_vals, w_gate, w_up, w_down):
    return pl.pallas_call(
        layer,
        out_shape=jax.ShapeDtypeStruct(resid.shape, BF),
        in_specs=[ANY, ANY, ANY, VM, VM, VM, ANY, ANY, ANY],
        out_specs=ANY,
        scratch_shapes=scratch(),
        compiler_params=pltpu.CompilerParams(
            collective_id=0, has_side_effects=True, vmem_limit_bytes=62 * 2**20
        ),
        name="layer",
    )(
        attn,
        w_out,
        resid,
        norm_gain.reshape(1, -1),
        route_ids.reshape(1, -1),
        gate_vals.reshape(1, -1),
        w_gate,
        w_up,
        w_down,
    )


def solution(mesh):
    placed = (
        P(("dp", "expert"), "tensor"),
        P("tensor", "expert"),
        P(("dp", "expert", "tensor"), None),
        P(),
        P(("dp", "expert", "tensor"), None),
        P(("dp", "expert", "tensor"), None),
        P("expert", None, "tensor"),
        P("expert", None, "tensor"),
        P("expert", "tensor", None),
    )
    return jax.shard_map(
        shards,
        mesh=mesh,
        in_specs=placed,
        out_specs=P(("dp", "expert", "tensor"), None),
        check_vma=False,
    )
```

time: 190 us -> 173 us (0.911)
  Pallas kernels: 187 us -> 171 us
    pallas_call x1, Pallas kernels: 187 us -> 171 us  [shards(): pl.pallas_call(layer, out_shape=jax.ShapeDtypeStruct(resid.shape, BF), in...]
where the time goes in v4:
time: 173 us
  Pallas kernels  171 us (99%)
  local copies, waits for them, and re-layouts  2.46 us (1%)
    pallas_call x1, Pallas kernels, shards(): pl.pallas_call(layer, out_shape=jax.ShapeDtypeStruct(resid.shape, BF), in...  171 us

profile of v4, /device:TPU:1, one launch (start us, length us, event | category | flops | bytes accessed | tf_op | source)
XLA Modules:
  0.0 173.2 jit_solution(14077257233969685347)
XLA Ops:
  0.0 170.7 %layer.1 = bf16[128,5120]{1,0:T(8,128)(2,1)} custom-call(bf16[512,2048]{1,0:T(8,128)(2,1)} %attn.1, bf16[2048,640]{1,0:T(8,128)(2,1)} %w_out.1, bf16[128,5120]{1,0:T(8,128)(2,1)} %resid.1, f32[1,5120]{1,0:T(1,128)} %bitcast.3, s32[1,128]{1,0:T(1,128)} %bitcast.4, f32[1,128]{1,0:T(1,128)} %bitcast.5, bf16[1,5120,384]{2,1,0:T(8,128)(2,1)} %w_gate.1, ...), custom_call_target="tpu_custom_call" | custom-call | tf_op jit(solution)/shard_map/layer/pallas_call | solution.py:766
  170.7 2.5 %copy.11 = bf16[128,5120]{1,0:T(8,128)(2,1)} copy(bf16[128,5120]{1,0:T(8,128)(2,1)} %layer.1) | data formatting | bytes 2621440

commit v5 on v4

--- a/solution.py
+++ b/solution.py
@@ -495,7 +495,6 @@
     def show_rows():
         shown.append(links.send(res.at[:, :, early], near.at[2], xp))
         shown.append(links.send(res.at[:, :, early], near.at[0], xm))
-        front["shown"] = shown[-1]
 
     def show_on_ahead():
         shown[0].wait_recv()
@@ -651,7 +650,6 @@
     def output(slot):
         if not stay:
             side["hid"].wait_recv()
-            links.settle_through(front["shown"])
         stay.append(slot)
         links.landed(land("out", slot), fin.at[0, 1 - c] if slot == 0 else fin.at[slot], sib)
         b = lax.rem(x + slot, 4)
@@ -659,12 +657,8 @@
         for half, rows in enumerate((hid.at[c], hid_sib)):
             core = c if half == 0 else 1 - c
             total = rows[:, cols] + weight * fin[slot, core].astype(F32)
-            res[core, :, cols] = total.astype(BF)
             col = pl.ds(pl.multiple_of((2 * b + core) * STRIP, 128), STRIP)
-            keep = pltpu.make_async_copy(
-                res.at[core, :, cols], out.at[:, col], local_sems.at[9]
-            )
-            keep.start()
+            out[:, col] = total.astype(BF)
 
     step(TO_SIBLING, start_sibling)
     step(DOWN_X, start_dn)
@@ -721,7 +715,6 @@
         steps.pop(key)()
     steps.pop((ACT_RELAY, LAST))
     assert not steps
-    pltpu.make_async_copy(out, out, local_sems.at[9]).wait()
     links.settle_all_but(0)
 
 
@@ -754,7 +747,7 @@
         pltpu.VMEM((4, 2, 128, STRIP), BF),
         pltpu.SemaphoreType.DMA((SENDS,)),
         pltpu.SemaphoreType.DMA((LANDINGS,)),
-        pltpu.SemaphoreType.DMA((10,)),
+        pltpu.SemaphoreType.DMA((9,)),
     ]
 
 
@@ -765,9 +758,9 @@
 def shards(attn, w_out, resid, norm_gain, route_ids, gate_vals, w_gate, w_up, w_down):
     return pl.pallas_call(
         layer,
-        out_shape=jax.ShapeDtypeStruct(resid.shape, BF),
+        out_shape=pltpu.VMEM(resid.shape, BF),
         in_specs=[ANY, ANY, ANY, VM, VM, VM, ANY, ANY, ANY],
-        out_specs=ANY,
+        out_specs=VM,
         scratch_shapes=scratch(),
         compiler_params=pltpu.CompilerParams(
             collective_id=0, has_side_effects=True, vmem_limit_bytes=62 * 2**20

time: 173 us -> 171 us (0.988)
  no operation moved by 1% of the time
where the time goes in v5:
time: 171 us
  Pallas kernels  170 us (99%)
    pallas_call x1, Pallas kernels, shards(): pl.pallas_call(layer, out_shape=pltpu.VMEM(resid.shape, BF), in_specs=[AN...  170 us

profile of v5, /device:TPU:1, one launch (start us, length us, event | category | flops | bytes accessed | tf_op | source)
XLA Modules:
  0.0 171.1 jit_solution(14406185352824487038)
XLA Ops:
  0.0 170.0 %layer.1 = bf16[128,5120]{1,0:T(8,128)(2,1)S(1)} custom-call(bf16[512,2048]{1,0:T(8,128)(2,1)} %attn.1, bf16[2048,640]{1,0:T(8,128)(2,1)} %w_out.1, bf16[128,5120]{1,0:T(8,128)(2,1)} %resid.1, f32[1,5120]{1,0:T(1,128)} %bitcast.3, s32[1,128]{1,0:T(1,128)} %bitcast.4, f32[1,128]{1,0:T(1,128)} %bitcast.5, bf16[1,5120,384]{2,1,0:T(8,128)(2,1)} %w_gate.1, ...), custom_call_target="tpu_custom_call" | custom-call | tf_op jit(solution)/shard_map/layer/pallas_call | solution.py:759
  170.0 1.1 copy.11

commit v6 on v5

--- a/solution.py
+++ b/solution.py
@@ -100,9 +100,9 @@
         )
 
 
-SENDS = 92
-LANDINGS = 167
-KEEP = 48
+SENDS = 80
+LANDINGS = 157
+KEEP = 36
 CAP = 24
 PAIR = 2 * CAP
 LAST = 3
@@ -216,8 +216,8 @@
 
     def send_d(j):
         return (
-            links.send(own(j, rows_d), w.at[j, 1, rows_d], yp),
-            links.send(own(j, rows_d), w.at[j, 0, rows_d], ym),
+            links.send(own(j, rows_d), w.at[j, 1, rows_d], yp, land(j, "d")),
+            links.send(own(j, rows_d), w.at[j, 0, rows_d], ym, land(j, "d")),
         )
 
     n = PIECES
@@ -344,9 +344,8 @@
         )
 
     def on_d(j):
-        d[j][0].wait_recv()
+        links.landed(land(j, "d"), w.at[j, pl.ds(0, 2), rows_d], yp)
         links.send(w.at[j, 1, rows_dh(0)], w.at[j, 2, rows_dh(0)], yp, land(j, "rd"))
-        d[j][1].wait_recv()
         links.send(w.at[j, 0, rows_dh(1)], w.at[j, 2, rows_dh(1)], ym, land(j, "rd"))
 
     def z_relay(j, pair, slot):
@@ -498,15 +497,14 @@
 
     def show_on_ahead():
         shown[0].wait_recv()
-        come[0] = links.send(near.at[2, 0], near.at[1, 0], xp)
+        come[0] = links.send(near.at[2, 0], near.at[1, 0], xp, land("near"))
 
     def show_on_behind():
         shown[1].wait_recv()
-        come[1] = links.send(near.at[0, 1], near.at[1, 1], xm)
+        come[1] = links.send(near.at[0, 1], near.at[1, 1], xm, land("near"))
 
     def wait_shown():
-        come[0].wait_recv()
-        come[1].wait_recv()
+        links.landed(land("near"), near.at[1], sib)
 
     def dispatch_shown(r, t):
         dy = (4 - r) % 4
@@ -540,17 +538,16 @@
 
     def relay_ahead(r):
         spread[r][0].wait_recv()
-        relay_x[r, 0] = links.send(rows_in.at[r, 3, 0, :, later], rows_in.at[r, 2, 0, :, later], xp)
+        relay_x[r, 0] = links.send(rows_in.at[r, 3, 0, :, later], rows_in.at[r, 2, 0, :, later], xp, land("relay", r))
 
     def relay_behind(r):
         spread[r][1].wait_recv()
-        relay_x[r, 1] = links.send(rows_in.at[r, 1, 1, :, later], rows_in.at[r, 2, 1, :, later], xm)
+        relay_x[r, 1] = links.send(rows_in.at[r, 1, 1, :, later], rows_in.at[r, 2, 1, :, later], xm, land("relay", r))
 
     act_x = {}
 
     def gate_up(r):
-        relay_x[r, 0].wait_recv()
-        relay_x[r, 1].wait_recv()
+        links.landed(land("relay", r), rows_in.at[r, 2, :, :, later], sib)
         links.settle_all_but(KEEP)
         both = jnp.dot(
             rows_in[r, :, 0].reshape(4 * PAIR, 4 * STRIP), w_gu[0], preferred_element_type=F32

time: 171 us -> 171 us (level)
  no operation moved by 1% of the time
where the time goes in v6:
time: 171 us
  Pallas kernels  170 us (99%)
    pallas_call x1, Pallas kernels, shards(): pl.pallas_call(layer, out_shape=pltpu.VMEM(resid.shape, BF), in_specs=[AN...  170 us

profile of v6, /device:TPU:1, one launch (start us, length us, event | category | flops | bytes accessed | tf_op | source)
XLA Modules:
  0.0 170.8 jit_solution(16036603520898179769)
XLA Ops:
  0.0 169.8 %layer.1 = bf16[128,5120]{1,0:T(8,128)(2,1)S(1)} custom-call(bf16[512,2048]{1,0:T(8,128)(2,1)} %attn.1, bf16[2048,640]{1,0:T(8,128)(2,1)} %w_out.1, bf16[128,5120]{1,0:T(8,128)(2,1)} %resid.1, f32[1,5120]{1,0:T(1,128)} %bitcast.3, s32[1,128]{1,0:T(1,128)} %bitcast.4, f32[1,128]{1,0:T(1,128)} %bitcast.5, bf16[1,5120,384]{2,1,0:T(8,128)(2,1)} %w_gate.1, ...), custom_call_target="tpu_custom_call" | custom-call | tf_op jit(solution)/shard_map/layer/pallas_call | solution.py:756
  169.8 1.1 copy.11
